TPU v7x, 512 devices: a whole 4x8x8 slice. The times are simulated.
512 devices in a mesh: dp: 32 (over x, z_lo, core), tm: 16 (over y, z_hi).
Axes of the slice: x: 4, y: 8, z: 8 (z_hi: 2, z_lo: 4; z = z_hi * 4 + z_lo), core: 2. Of those that a mesh axis runs over, the one named last changes fastest.
Arguments:
- video: bfloat16 [32, 64, 64, 640], P('dp', 'tm'), may hold values from -6 to 6
- cotangent: bfloat16 [32, 64, 64, 640], P('dp', 'tm'), may hold values from -6 to 6
- spatial_weight: bfloat16 [9, 640, 640], P(None, 'tm'), may hold values from -0.078125 to 0.078125
- temporal_weight: bfloat16 [3, 640, 640], replicated, may hold values from -0.125 to 0.125
- proj_weight: bfloat16 [640, 640], replicated, may hold values from -0.25 to 0.25
Outputs:
- block_out: bfloat16 [32, 64, 64, 640], P('dp', 'tm')
- video_grad: bfloat16 [32, 64, 64, 640], P('dp', 'tm')
- proj_grad: float32 [640, 640], P('tm')
All inputs are finite; a program needn't handle non-finite values.
Results may differ from a plain program's by a relative error of at most 0.03.
Values may be sent and summed in bfloat16 or wider, within the bound.
No kernel may reach another device: no remote copies, remote signals or barrier semaphores. Data moves between devices by JAX's collectives and lax.ppermute only.
A program may use at most 64 MiB of HBM per device.

v0:
```python
import math

import jax
import jax.numpy as jnp
from jax import lax
from jax.sharding import PartitionSpec as P

HGT = 8
WID = 8


def silu_grad(values):
    sigmoid = jax.nn.sigmoid(values)
    return sigmoid * (1.0 + values * (1.0 - sigmoid))


def patches(volume, orient):
    grid_rows, grid_cols = (volume.shape[2], volume.shape[3])
    padded = jnp.pad(volume, ((0, 0), (0, 0), (1, 1), (1, 1), (0, 0)))
    pieces = []
    for row_off in (-1, 0, 1):
        for col_off in (-1, 0, 1):
            row_start = 1 + orient * row_off
            col_start = 1 + orient * col_off
            pieces.append(
                padded[
                    :, :, row_start : row_start + grid_rows, col_start : col_start + grid_cols, :
                ]
            )
    return jnp.stack(pieces, axis=4)


def temporal_forward(extended, weight, frame_count):
    stacked = jnp.stack(
        [
            lax.slice_in_dim(extended, 2 * tap_index, 2 * tap_index + frame_count, axis=1)
            for tap_index in range(3)
        ],
        axis=3,
    )
    return jnp.einsum("bfqmc,mco->bfqo", stacked, weight, preferred_element_type=jnp.float32)


def temporal_backward(extended, weight, frame_count):
    stacked = jnp.stack(
        [
            lax.slice_in_dim(extended, 4 - 2 * tap_index, 4 - 2 * tap_index + frame_count, axis=1)
            for tap_index in range(3)
        ],
        axis=3,
    )
    return jnp.einsum("bfqmo,mco->bfqc", stacked, weight, preferred_element_type=jnp.float32)


def pad_frames(tiles):
    return jnp.pad(tiles, ((0, 0), (2, 2), (0, 0), (0, 0)))


def local(video, cotangent, spatial_weight, temporal_weight, proj_weight):
    clip_count, frame_count, pos_count, channels = video.shape
    row_count = clip_count * frame_count * pos_count
    volume = video.reshape(clip_count, frame_count, HGT, WID, channels)
    act = jax.nn.silu(volume.astype(jnp.float32)).astype(jnp.bfloat16)
    act_patches = patches(act, 1).reshape(row_count, 9, channels)
    shard_piece = lax.all_gather(spatial_weight, "tm", axis=1, tiled=True)
    accumulated = jnp.einsum(
        "rtk,tko->ro", act_patches, shard_piece, preferred_element_type=jnp.float32
    )
    spatial = accumulated.astype(jnp.bfloat16).reshape(clip_count, frame_count, pos_count, channels)
    tiles = lax.all_to_all(spatial, "tm", split_axis=2, concat_axis=1, tiled=True)
    mixed = temporal_forward(pad_frames(tiles), temporal_weight, tiles.shape[1]).astype(
        jnp.bfloat16
    )
    temporal = lax.all_to_all(mixed, "tm", split_axis=1, concat_axis=2, tiled=True)
    temporal_rows = temporal.reshape(row_count, channels).astype(jnp.float32)
    gated = jax.nn.silu(temporal_rows).astype(jnp.bfloat16)
    branch = jnp.dot(gated, proj_weight, preferred_element_type=jnp.float32)
    in_rows = video.reshape(row_count, channels).astype(jnp.float32)
    block_out = (in_rows + branch).astype(jnp.bfloat16).reshape(video.shape)
    grad_rows = cotangent.reshape(row_count, channels)
    back_proj = lax.dot_general(
        grad_rows, proj_weight, (((1,), (1,)), ((), ())), preferred_element_type=jnp.float32
    )
    gated_grad = (
        (back_proj * silu_grad(temporal_rows))
        .astype(jnp.bfloat16)
        .reshape(clip_count, frame_count, pos_count, channels)
    )
    tiles = lax.all_to_all(gated_grad, "tm", split_axis=2, concat_axis=1, tiled=True)
    mixed = temporal_backward(pad_frames(tiles), temporal_weight, tiles.shape[1]).astype(
        jnp.bfloat16
    )
    spatial_grad = lax.all_to_all(mixed, "tm", split_axis=1, concat_axis=2, tiled=True)
    grad_volume = spatial_grad.reshape(clip_count, frame_count, HGT, WID, channels)
    grad_patches = patches(grad_volume, -1).reshape(row_count, 9, channels)
    act_grad = jnp.einsum(
        "rto,tko->rk", grad_patches, shard_piece, preferred_element_type=jnp.float32
    )
    video_grad = (
        (grad_rows.astype(jnp.float32) + act_grad * silu_grad(in_rows))
        .astype(jnp.bfloat16)
        .reshape(video.shape)
    )
    partial_value = lax.dot_general(
        gated, grad_rows, (((0,), (0,)), ((), ())), preferred_element_type=jnp.float32
    )
    row_share = lax.psum_scatter(
        partial_value.astype(jnp.bfloat16), "tm", scatter_dimension=0, tiled=True
    )
    summed = lax.psum(row_share, "dp").astype(jnp.float32)
    factor = 1.0 / math.sqrt(row_count * lax.axis_size("dp") * lax.axis_size("tm"))
    return (block_out, video_grad, summed * factor)


def solution(mesh):
    in_specs = (P("dp", "tm", None, None), P("dp", "tm", None, None), P(None, "tm", None), P(), P())
    out_specs = (P("dp", "tm", None, None), P("dp", "tm", None, None), P("tm", None))
    return jax.shard_map(local, mesh=mesh, in_specs=in_specs, out_specs=out_specs, check_vma=False)
```

profile of v0, /device:TPU:16, one launch (start us, length us, event | category | flops | bytes accessed | tf_op | source)
XLA Modules:
  0.0 589.2 jit_solution(402093575774485815)
XLA Ops:
  7.9 1.2 fusion.47
  16.5 177.8 %all-gather.2.cloned.1.call-done = bf16[9,640,640]{2,1,0:T(8,128)(2,1)} async-done(((bf16[9,40,640]{2,1,0:T(8,128)(2,1)}), bf16[9,640,640]{2,1,0:T(8,128)(2,1)}) %all-gather.2.cloned.1.call-update) | async-done | bytes 7372816 | tf_op jit(solution)/shard_map/all_gather | solution.py:65
  194.2 6.5 %fusion.12 = bf16[256,640]{1,0:T(8,128)(2,1)S(1)} fusion(bf16[256,9,640]{2,0,1:T(8,128)(2,1)} %constant_dynamic-update-slice_fusion, bf16[9,640,640]{2,1,0:T(8,128)(2,1)} %all-gather.2.cloned.1.call-done), kind=kOutput, calls=%fused_computation.21 | convolution fusion | flops 1887600640 | bytes 10649600 | tf_op jit(solution)/shard_map/rtk,tko->ro/dot_general | solution.py:66
  201.0 20.4 %all_to_all.60 = bf16[1,4,64,640]{3,1,0,2:T(4,128)(2,1)S(1)} all-to-all(bf16[1,4,64,640]{3,1,0,2:T(4,128)(2,1)S(1)} %copy.29), channel_id=1, replica_groups=mesh['dp'=32,'tm'=16] {'tm'}, dimensions={2} | all-to-all | bytes 655360 | tf_op jit(solution)/shard_map/all_to_all | solution.py:70
  222.5 1.9 fusion.22
  224.7 19.2 %all_to_all.61 = bf16[1,64,4,640]{3,2,0,1:T(4,128)(2,1)S(1)} all-to-all(bf16[1,64,4,640]{3,2,0,1:T(4,128)(2,1)S(1)} %copy.32), channel_id=1, replica_groups=mesh['dp'=32,'tm'=16] {'tm'}, dimensions={1} | all-to-all | bytes 655360 | tf_op jit(solution)/shard_map/all_to_all | solution.py:74
  244.0 1.0 copy_bitcast_fusion
  244.9 2.1 reshape.168
  247.1 1.8 fusion.14
  248.9 1.0 copy.34
  249.9 5.3 all-to-all-start.2
  255.1 1.1 fusion.46
  256.2 12.3 %all-to-all-done.2 = bf16[1,4,64,640]{3,1,0,2:T(4,128)(2,1)S(1)} async-done(((bf16[1,4,64,640]{3,1,0,2:T(4,128)(2,1)}), bf16[1,4,64,640]{3,1,0,2:T(4,128)(2,1)S(1)}, u32[]{:S(2)}, u32[]{:S(2)}) %all-to-all-start.2) | async-done | bytes 327712 | tf_op jit(solution)/shard_map/all_to_all | solution.py:89
  269.3 1.1 copy.57
  272.0 1.3 fusion.52
  273.2 2.0 fusion.25
  275.2 1.0 copy.37
  276.2 5.4 all-to-all-start.3
  281.8 1.1 fusion.49
  282.9 1.1 convert_element_type.142
  283.9 2.3 convolution_convert_fusion
  286.3 2.6 fusion.13
  288.9 6.2 %all-to-all-done.3 = bf16[1,64,4,640]{3,2,0,1:T(4,128)(2,1)S(1)} async-done(((bf16[1,64,4,640]{3,2,0,1:T(4,128)(2,1)}), bf16[1,64,4,640]{3,2,0,1:T(4,128)(2,1)S(1)}, u32[]{:S(2)}, u32[]{:S(2)}) %all-to-all-start.3) | async-done | bytes 327712 | tf_op jit(solution)/shard_map/all_to_all | solution.py:93
  295.2 1.7 pad_slice_fusion.12
  299.4 1.8 stack.103
  301.2 1.1 copy.44
  302.3 1.0 copy.45
  303.4 1.1 copy.46
  304.5 1.0 copy.47
  310.9 7.3 %fusion.21 = bf16[256,640]{1,0:T(8,128)(2,1)} fusion(f32[256,640]{1,0:T(8,128)S(1)} %copy-done.4, bf16[256,9,640]{2,0,1:T(8,128)(2,1)} %constant_dynamic-update-slice_fusion.9, bf16[9,640,640]{2,1,0:T(8,128)(2,1)} %all-gather.2.cloned.1.call-done, bf16[256,640]{1,0:T(8,128)(2,1)S(1)} %bitcast.198), kind=kOutput, calls=%fused_computation.26 | convolution fusion | flops 1888092160 | bytes 11632640 | tf_op jit(solution)/shard_map/rto,tko->rk/dot_general | solution.py:96
  318.1 130.2 %reduce-scatter.4.cloned.1.call-done = bf16[40,640]{1,0:T(8,128)(2,1)} async-done(((bf16[640,640]{1,0:T(8,128)(2,1)}), bf16[40,640]{1,0:T(8,128)(2,1)}) %reduce-scatter.4.cloned.1.call-update) | async-done | bytes 51216
  448.3 133.4 %psum.7 = bf16[40,640]{1,0:T(8,128)(2,1)S(1)} all-reduce(bf16[40,640]{1,0:T(8,128)(2,1)} %reduce-scatter.4.cloned.1.call-done), channel_id=1, replica_groups=mesh['dp'=32,'tm'=16] {'dp'}, use_global_device_ids=true, to_apply=%region_1.2 | all-reduce | flops 25600 | bytes 102400 | tf_op jit(solution)/shard_map/psum | solution.py:110
  (52 shorter events, 21.0 us)
Async XLA Ops:
  7.2 215.4 %copy-start = (bf16[3,640,640]{2,1,0:T(8,128)(2,1)S(1)}, bf16[3,640,640]{2,1,0:T(8,128)(2,1)}, u32[]{:S(2)}) copy-start(bf16[3,640,640]{2,1,0:T(8,128)(2,1)} %param.8) | copy-start | bytes 7372804
  7.2 187.1 %all-gather.2.cloned.1.call-start = ((), (), s32[]{:S(2)}) async-start(), calls=%async_computation.5 | async-start | bytes 7833600 | tf_op jit(solution)/shard_map/all_gather | solution.py:65
  9.1 3.4 copy-start.1
  224.5 22.6 %copy-start.5 = (bf16[1,4,64,640]{3,2,1,0:T(8,128)(2,1)S(1)}, bf16[1,4,64,640]{3,2,1,0:T(8,128)(2,1)}, u32[]{:S(2)}) copy-start(bf16[1,4,64,640]{3,2,1,0:T(8,128)(2,1)} %param.6) | copy-start | bytes 983044
  249.9 18.7 %all-to-all-start.2 = ((bf16[1,4,64,640]{3,1,0,2:T(4,128)(2,1)}), bf16[1,4,64,640]{3,1,0,2:T(4,128)(2,1)S(1)}, u32[]{:S(2)}, u32[]{:S(2)}) async-start(bf16[1,4,64,640]{3,1,0,2:T(4,128)(2,1)} %copy.34), calls=%async_computation.2 | async-start | bytes 655360 | tf_op jit(solution)/shard_map/all_to_all | solution.py:89
  268.5 0.7 copy-start.3
  276.2 18.9 %all-to-all-start.3 = ((bf16[1,64,4,640]{3,2,0,1:T(4,128)(2,1)}), bf16[1,64,4,640]{3,2,0,1:T(4,128)(2,1)S(1)}, u32[]{:S(2)}, u32[]{:S(2)}) async-start(bf16[1,64,4,640]{3,2,0,1:T(4,128)(2,1)} %copy.37), calls=%async_computation.3 | async-start | bytes 655360 | tf_op jit(solution)/shard_map/all_to_all | solution.py:93
  281.6 166.7 %reduce-scatter.4.cloned.1.call-start = ((), (), s32[]{:S(2)}) async-start(), calls=%async_computation.6 | async-start | bytes 870400
  301.2 5.8 copy-start.2
  303.3 7.5 %copy-start.4 = (f32[256,640]{1,0:T(8,128)S(1)}, f32[256,640]{1,0:T(8,128)}, u32[]{:S(2)}) copy-start(f32[256,640]{1,0:T(8,128)} %fusion.46) | copy-start | bytes 1966084
  303.3 7.5 %copy-start.6 = (bf16[1,4,64,640]{3,2,1,0:T(8,128)(2,1)S(1)}, bf16[1,4,64,640]{3,2,1,0:T(8,128)(2,1)}, u32[]{:S(2)}) copy-start(bf16[1,4,64,640]{3,2,1,0:T(8,128)(2,1)} %param.6) | copy-start | bytes 983044
Sparse Core Ops, SparseCore 0:
  11.2 182.9 all-gather.1
  286.8 161.4 reduce-scatter.3
where the time goes:
time: 590 us; the launch traced here: 589 us
  waiting for transfers between devices  327 us (55%)
  blocking collectives  173 us (29%)
  local copies, waits for them, and re-layouts  33.6 us (6%)
  matrix products  24.4 us (4%)
  between operations  14.2 us (2%)
  starting transfers between devices  10.9 us (2%)
    all_gather x1, waiting for transfers between devices, local(): shard_piece = lax.all_gather(spatial_weight, 'tm', axis=1, tiled=True)  178 us
    psum x1, blocking collectives, local(): summed = lax.psum(row_share, 'dp').astype(jnp.float32)  133 us
    unnamed x3, waiting for transfers between devices  131 us
    all_to_all x1, blocking collectives, local(): lax.all_to_all(spatial, 'tm', split_axis=2, concat_axis=1, tiled=True)  20.4 us
    all_to_all x1, blocking collectives, local(): lax.all_to_all(mixed, 'tm', split_axis=1, concat_axis=2, tiled=True)  19.2 us
    all_to_all x1, waiting for transfers between devices, local(): lax.all_to_all(gated_grad, 'tm', split_axis=2, concat_axis=1, tiled=True)  12.3 us
    unnamed x29, local copies, waits for them, and re-layouts  12.3 us
  transfers between devices with their start and end apart: 4, of which 4 were waited for; matrix products, arithmetic and copies ran while one was open for 7% of the time, Pallas kernels for 0%

commit v1 on v0

v1 whole, which is shorter than its diff:
```python
import functools
import math

import jax
import jax.numpy as jnp
from jax import lax
from jax.experimental import pallas as pl
from jax.experimental.pallas import tpu as pltpu
from jax.sharding import Mesh
from jax.sharding import PartitionSpec as P

C = 640
ROWS = 256
HALO = 128
EXT = ROWS + 2 * HALO
PIECE = 768
HALF = PIECE // 2
LEFT = 384
TAIL = PIECE - C
PIECES = 8
TM = 16
SHARD = 40
VMEM = 50 * 1024 * 1024
F32 = jnp.float32
BF16 = jnp.bfloat16
TAPS = [(di, dj) for di in (-1, 0, 1) for dj in (-1, 0, 1)]


def sigmoid(values):
    return 1.0 / (1.0 + jnp.exp(-values))


def silu_grad(values):
    s = sigmoid(values)
    return s * (1.0 + values * (1.0 - s))


def shifted(values, di, dj):
    rows = values.shape[0]
    step = 8 * di + dj
    moved = values if step == 0 else pltpu.roll(values, (-step) % rows, 0)
    if step == 0:
        return moved
    row = lax.broadcasted_iota(jnp.int32, values.shape, 0)
    i = (row // 8) % 8 + di
    j = row % 8 + dj
    inside = (i >= 0) & (i < 8) & (j >= 0) & (j < 8)
    return jnp.where(inside, moved, 0.0)


def prep_kernel(video_ref, spread_ref, out_ref):
    x = video_ref[...].astype(F32)
    act = (x * sigmoid(x)).astype(BF16).astype(F32)
    last = shifted(act, *TAPS[8]).astype(BF16)
    tail = jnp.dot(last, spread_ref[...], preferred_element_type=F32).astype(BF16)
    for tap in range(PIECES):
        out_ref[tap, :, :C] = shifted(act, *TAPS[tap]).astype(BF16)
        out_ref[tap, :, C:] = tail[:, tap * TAIL : (tap + 1) * TAIL]


def prep(video_ext, spread):
    chunk = 128
    return pl.pallas_call(
        prep_kernel,
        grid=(EXT // chunk,),
        in_specs=[
            pl.BlockSpec((chunk, C), lambda n: (n, 0)),
            pl.BlockSpec((C, PIECES * TAIL), lambda n: (0, 0)),
        ],
        out_specs=pl.BlockSpec((PIECES, chunk, PIECE), lambda n: (0, n, 0)),
        out_shape=jax.ShapeDtypeStruct((PIECES, EXT, PIECE), BF16),
        compiler_params=pltpu.CompilerParams(vmem_limit_bytes=VMEM),
        cost_estimate=pl.CostEstimate(flops=2 * EXT * C * PIECES * TAIL, bytes_accessed=20 * 1024 * 1024, transcendentals=0),
        name="patches",
    )(video_ext, spread)


def weight_copies(place_ref, refs, which, held, sems, index):
    quarter, start = place_ref[0], place_ref[2]
    first, second = refs
    copies = []
    for n in range(4):
        left = (start + n) % 4
        right = (quarter + n) % 4
        pair = (
            pltpu.make_async_copy(
                first.at[n], held.at[index(left, which), :, pl.ds(0, LEFT)], sems.at[2 * n]
            ),
            pltpu.make_async_copy(
                second.at[n], held.at[index(right, which), :, pl.ds(LEFT, C - LEFT)], sems.at[2 * n + 1]
            ),
        )
        for copy in pair:
            copy.start()
        copies += pair
    return copies


def spatial_sum(patch_ref, which, patches, patch_sems, held, copies):
    patch_copies = []
    for quarter in range(4):
        copy = pltpu.make_async_copy(
            patch_ref.at[2 * quarter + which], patches.at[quarter], patch_sems.at[quarter]
        )
        copy.start()
        patch_copies.append(copy)
    for copy in copies + patch_copies:
        copy.wait()
    value = jnp.dot(patches[0], held[0], preferred_element_type=F32)
    for quarter in range(1, 4):
        value += jnp.dot(patches[quarter], held[quarter], preferred_element_type=F32)
    return value


def one_core(quarter, which):
    return quarter


def both_cores(quarter, which):
    return 2 * quarter + which


def partial_kernel(place_ref, first, second, patch_ref, out_ref, held, patches, sems, patch_sems):
    core = place_ref[1]
    copies = weight_copies(place_ref, (first, second), core, held, sems, one_core)
    out_ref[...] = spatial_sum(patch_ref, core, patches, patch_sems, held, copies)


def forward_kernel(place_ref, first, second, patch_ref, *refs):
    partial_ref, video_ref, cot_ref, temporal_ref, proj_ref, order_ref = refs[:6]
    block_ref, gg_ref, keep_ref, give_ref = refs[6:10]
    held, patches, sems, patch_sems = refs[10:]
    core = 1 - place_ref[1]
    copies = weight_copies(place_ref, (first, second), core, held, sems, one_core)
    total = spatial_sum(patch_ref, core, patches, patch_sems, held, copies) + partial_ref[...]
    spatial = total.astype(BF16)
    temporal = jnp.dot(spatial[:ROWS], temporal_ref[0], preferred_element_type=F32)
    for m in (1, 2):
        temporal += jnp.dot(
            spatial[m * HALO : m * HALO + ROWS], temporal_ref[m], preferred_element_type=F32
        )
    temporal = temporal.astype(BF16).astype(F32)
    s = sigmoid(temporal)
    gated = (temporal * s).astype(BF16)
    cot = cot_ref[...]
    ordered = jnp.dot(gated, order_ref[...], preferred_element_type=F32).astype(BF16)
    part = lax.dot_general(
        ordered, cot, (((0,), (0,)), ((), ())), preferred_element_type=F32
    ).astype(BF16)
    keep_ref[...] = part[:HALF]
    give_ref[...] = part[HALF:]
    back = lax.dot_general(
        cot, proj_ref[...], (((1,), (1,)), ((), ())), preferred_element_type=F32
    )
    gg_ref[...] = (back * (s * (1.0 + temporal * (1.0 - s)))).astype(BF16)
    branch = jnp.dot(gated, proj_ref[...], preferred_element_type=F32)
    block_ref[...] = (video_ref[...].astype(F32) + branch).astype(BF16)


def backward_kernel(place_ref, first, second, other_first, other_second, *refs):
    ext_ref, video_ref, cot_ref, temporal_ref, spread_ref = refs[:5]
    out_ref = refs[5]
    held, tail, total, sems, other_sems = refs[6:]
    core = place_ref[1]
    copies = weight_copies(place_ref, (first, second), core, held, sems, both_cores)
    copies += weight_copies(
        place_ref, (other_first, other_second), 1 - core, held, other_sems, both_cores
    )
    ext = ext_ref[...]
    nt = (((1,), (1,)), ((), ()))
    grad = lax.dot_general(ext[2 * HALO :], temporal_ref[0], nt, preferred_element_type=F32)
    grad += lax.dot_general(
        ext[HALO : HALO + ROWS], temporal_ref[1], nt, preferred_element_type=F32
    )
    grad += lax.dot_general(ext[:ROWS], temporal_ref[2], nt, preferred_element_type=F32)
    grad = grad.astype(BF16).astype(F32)
    for copy in copies:
        copy.wait()
    last = shifted(grad, -TAPS[8][0], -TAPS[8][1]).astype(BF16)
    for tap in range(PIECES):
        moved = shifted(grad, -TAPS[tap][0], -TAPS[tap][1]).astype(BF16)
        value = lax.dot_general(moved, held[tap, :C], nt, preferred_element_type=F32)
        if tap == 0:
            total[...] = value
        else:
            total[...] += value
        tail[:, tap * TAIL : (tap + 1) * TAIL] = lax.dot_general(
            last, held[tap, C:], nt, preferred_element_type=F32
        ).astype(BF16)
    total[...] += lax.dot_general(tail[...], spread_ref[...], nt, preferred_element_type=F32)
    video = video_ref[...].astype(F32)
    out_ref[...] = (
        cot_ref[...].astype(F32) + total[...] * silu_grad(video)
    ).astype(BF16)


def whole():
    return pl.BlockSpec(memory_space=pltpu.VMEM)


def anywhere():
    return pl.BlockSpec(memory_space=pl.ANY)


def partial(place, weights, patches):
    return pl.pallas_call(
        partial_kernel,
        in_specs=[pl.BlockSpec(memory_space=pltpu.SMEM)] + [anywhere()] * 3,
        out_specs=whole(),
        out_shape=jax.ShapeDtypeStruct((EXT, C), F32),
        scratch_shapes=[
            pltpu.VMEM((4, PIECE, C), BF16),
            pltpu.VMEM((4, EXT, PIECE), BF16),
            pltpu.SemaphoreType.DMA((8,)),
            pltpu.SemaphoreType.DMA((4,)),
        ],
        compiler_params=pltpu.CompilerParams(vmem_limit_bytes=VMEM),
        cost_estimate=pl.CostEstimate(
            flops=EXT * PIECES * PIECE * C, bytes_accessed=8 * 1024 * 1024, transcendentals=0
        ),
        name="partial",
    )(place, *weights, patches)


def forward(place, weights, patches, summed, video, cot, temporal_weight, proj_weight, order):
    return pl.pallas_call(
        forward_kernel,
        in_specs=[pl.BlockSpec(memory_space=pltpu.SMEM)] + [anywhere()] * 3 + [whole()] * 6,
        out_specs=[whole()] * 4,
        out_shape=[
            jax.ShapeDtypeStruct((ROWS, C), BF16),
            jax.ShapeDtypeStruct((ROWS, C), BF16),
            jax.ShapeDtypeStruct((HALF, C), BF16),
            jax.ShapeDtypeStruct((HALF, C), BF16),
        ],
        scratch_shapes=[
            pltpu.VMEM((4, PIECE, C), BF16),
            pltpu.VMEM((4, EXT, PIECE), BF16),
            pltpu.SemaphoreType.DMA((8,)),
            pltpu.SemaphoreType.DMA((4,)),
        ],
        compiler_params=pltpu.CompilerParams(vmem_limit_bytes=VMEM),
        cost_estimate=pl.CostEstimate(
            flops=2 * EXT * PIECES * PIECE * C, bytes_accessed=20 * 1024 * 1024, transcendentals=0
        ),
        name="forward",
    )(place, *weights, patches, summed, video, cot, temporal_weight, proj_weight, order)


def backward(place, weights, ext, video, cot, temporal_weight, spread):
    return pl.pallas_call(
        backward_kernel,
        in_specs=[pl.BlockSpec(memory_space=pltpu.SMEM)] + [anywhere()] * 4 + [whole()] * 5,
        out_specs=whole(),
        out_shape=jax.ShapeDtypeStruct((ROWS, C), BF16),
        scratch_shapes=[
            pltpu.VMEM((PIECES, PIECE, C), BF16),
            pltpu.VMEM((ROWS, PIECES * TAIL), BF16),
            pltpu.VMEM((ROWS, C), F32),
            pltpu.SemaphoreType.DMA((8,)),
            pltpu.SemaphoreType.DMA((8,)),
        ],
        compiler_params=pltpu.CompilerParams(vmem_limit_bytes=VMEM),
        cost_estimate=pl.CostEstimate(
            flops=2 * ROWS * PIECES * PIECE * C, bytes_accessed=30 * 1024 * 1024, transcendentals=0
        ),
        name="backward",
    )(place, *weights, ext, video, cot, temporal_weight, spread)


def next_quarter(values, r):
    def step(c):
        return (0, 1, 2 if c == 0 else -2, -1)[r]

    pairs = [(c * 8 + (y + step(c)) % 8, c * 8 + y) for y in range(8) for c in range(2)]
    return lax.ppermute(values, ("c", "y"), pairs)


def paired(values):
    groups = [
        [(zl if zh == 0 else 3 - zl) * 16 + y * 2 + zh for y in range(8) for zh in range(2)]
        for zl in range(4)
    ]
    return lax.all_to_all(
        values, ("zl", "y", "zh"), split_axis=0, concat_axis=0, axis_index_groups=groups, tiled=True
    )


def other_core(values):
    return lax.ppermute(values, "c", [(0, 1), (1, 0)])


def halos(rows):
    tm = ("y", "zh")
    before = lax.ppermute(rows[ROWS - HALO :], tm, [(t, t + 1) for t in range(TM - 1)])
    after = lax.ppermute(rows[:HALO], tm, [(t + 1, t) for t in range(TM - 1)])
    return before, after


def spread_matrix():
    k = lax.broadcasted_iota(jnp.int32, (C, PIECES * TAIL), 0)
    lane = lax.broadcasted_iota(jnp.int32, (C, PIECES * TAIL), 1)
    j, t, i = lane // TAIL, (lane % TAIL) // 8, lane % 8
    return ((i < 5) & (k == SHARD * t + 5 * j + i)).astype(BF16)


def order_matrix(core):
    k = lax.broadcasted_iota(jnp.int32, (C, PIECE), 0)
    lane = lax.broadcasted_iota(jnp.int32, (C, PIECE), 1)
    h, t, i = (lane // HALF + core) % 2, (lane % HALF) // 24, lane % 24
    return ((i < 20) & (k == SHARD * t + 20 * h + i)).astype(BF16)


def local(video, cotangent, spatial_weight, temporal_weight, proj_weight):
    core = lax.axis_index("c")
    x, y, zl, zh = (lax.axis_index(name) for name in ("x", "y", "zl", "zh"))
    quarter = (x + y + zl) % 4
    place = jnp.stack([quarter, core, (y + zl) % 4]).astype(jnp.int32)

    rows = video.reshape(ROWS, C)
    cot = cotangent.reshape(ROWS, C)

    main = spatial_weight[:8].reshape(4, 2, SHARD, C)
    tail = spatial_weight[8].reshape(4, 2, 5, C)
    main = lax.dynamic_index_in_dim(main, core, 1, keepdims=False)
    tail = lax.dynamic_index_in_dim(tail, core, 1, keepdims=False)
    quarters = jnp.concatenate([main, tail, jnp.zeros((4, 3, C), BF16)], axis=1)
    quarters = jnp.concatenate([quarters, quarters], axis=0)
    low = lax.dynamic_slice_in_dim(quarters, (x + jnp.where(zh == 0, zl, 3 - zl)) % 4, 4, 0)
    high = lax.dynamic_slice_in_dim(quarters, (x + jnp.where(zh == 0, 3 - zl, zl)) % 4, 4, 0)
    sent = jnp.stack([low, high], axis=1)
    sent = jnp.broadcast_to(sent[None], (2, 4, 2, 48, C)).reshape(TM, 48, C)

    def rowed(got):
        width = got.shape[2]
        return jnp.concatenate(
            [got[:, :SHARD].reshape(C, width), got[:, SHARD:].reshape(TAIL, width)], axis=0
        )

    got, shared = lax.optimization_barrier((paired(sent), rows))
    left, right = rowed(got[:, :, :LEFT]), rowed(got[:, :, LEFT:])
    first = lax.all_to_all(
        jnp.broadcast_to(left[None], (4, PIECE, LEFT)), "x", split_axis=0, concat_axis=0, tiled=True
    )
    second = [right] + [next_quarter(right, r) for r in (1, 2, 3)]
    before, after = halos(shared)
    spread = spread_matrix()
    patches = prep(jnp.concatenate([before, rows, after], axis=0), spread)
    first, patches, *second = lax.optimization_barrier((first, patches, *second))
    weights = [first, jnp.stack(second)]
    others = [other_core(v) for v in weights]

    summed = partial(place, weights, patches)
    block_out, gated_grad, keep, give = forward(
        place, others, patches, summed, rows, cot, temporal_weight, proj_weight, order_matrix(core)
    )

    before, after = halos(gated_grad)
    pair = (keep.astype(F32) + other_core(give).astype(F32)).astype(BF16)
    blocks = paired(pair.reshape(TM, 24, C))
    blocks, before, after = lax.optimization_barrier((blocks, before, after))
    ext = jnp.concatenate([before, gated_grad, after], axis=0)
    video_grad = backward(place, weights + others, ext, rows, cot, temporal_weight, spread)

    block = jnp.sum(blocks.astype(F32), axis=0).astype(BF16)
    sent = jnp.broadcast_to(block[None], (16, 24, C))
    copies = lax.all_to_all(sent, ("x", "zl"), split_axis=0, concat_axis=0, tiled=True)
    copies, video_grad = lax.optimization_barrier((copies, video_grad))
    summed = jnp.sum(copies.astype(F32), axis=0)
    theirs = other_core(summed)
    low = jnp.where(core == 0, summed, theirs)[:20]
    high = jnp.where(core == 0, theirs, summed)[:20]
    factor = 1.0 / math.sqrt(ROWS * 512)
    proj_grad = jnp.concatenate([low, high], axis=0) * factor
    return (block_out.reshape(video.shape), video_grad.reshape(video.shape), proj_grad)


def solution(mesh):
    fine = Mesh(mesh.devices.reshape(4, 4, 2, 8, 2), ("x", "zl", "c", "y", "zh"))
    dp, tm = ("x", "zl", "c"), ("y", "zh")
    in_specs = (P(dp, tm, None, None), P(dp, tm, None, None), P(None, tm, None), P(), P())
    out_specs = (P(dp, tm, None, None), P(dp, tm, None, None), P(tm, None))
    return jax.shard_map(local, mesh=fine, in_specs=in_specs, out_specs=out_specs, check_vma=False)
```

time: 590 us -> 189 us (0.32)
  the two profiles are of different devices: /device:TPU:16 before, /device:TPU:25 now
where the time goes in v1:
time: 189 us; the launch traced here: 188 us
  starting transfers between devices  79.9 us (42%)
  waiting for transfers between devices  63 us (33%)
  Pallas kernels  31.9 us (17%)
  local copies, waits for them, and re-layouts  6.69 us (4%)
  other arithmetic  5.65 us (3%)
    all_to_all x2, waiting for transfers between devices, paired(): lax.all_to_all(values, ('zl', 'y', 'zh'), split_axis=0, concat_axis=0, ax...  29.1 us
    all_to_all x2, starting transfers between devices, paired(): lax.all_to_all(values, ('zl', 'y', 'zh'), split_axis=0, concat_axis=0, ax...  21.1 us
    ppermute x2, waiting for transfers between devices, halos(): lax.ppermute(rows[ROWS - HALO:], tm, [(t, t + 1) for t in range(TM - 1)])  18.3 us
    ppermute x2, starting transfers between devices, halos(): after = lax.ppermute(rows[:HALO], tm, [(t + 1, t) for t in range(TM - 1)])  15.7 us
    all_to_all x1, starting transfers between devices, local(): lax.all_to_all(sent, ('x', 'zl'), split_axis=0, concat_axis=0, tiled=True)  14.4 us
    pallas_call x1, Pallas kernels, forward(): pl.pallas_call(forward_kernel, in_specs=[pl.BlockSpec(memory_space=pltpu....  10.9 us
    pallas_call x1, Pallas kernels, backward(): pl.pallas_call(backward_kernel, in_specs=[pl.BlockSpec(memory_space=pltpu...  10.8 us
    ppermute x4, starting transfers between devices, other_core(): return lax.ppermute(values, 'c', [(0, 1), (1, 0)])  10.5 us
  transfers between devices with their start and end apart: 15, of which 8 were waited for; matrix products, arithmetic and copies ran while one was open for 2% of the time, Pallas kernels for 11%

profile of v1, /device:TPU:25, one launch (start us, length us, event | category | flops | bytes accessed | tf_op | source)
XLA Modules:
  0.0 188.3 jit_solution(402640029110722151)
XLA Ops:
  1.5 1.0 slice.42
  2.8 1.0 broadcast_in_dim.9
  3.9 15.3 %all-to-all-start = ((bf16[16,48,640]{2,1,0:T(8,128)(2,1)}), bf16[16,48,640]{2,1,0:T(8,128)(2,1)S(1)}, u32[]{:S(2)}, u32[]{:S(2)}) async-start(bf16[16,48,640]{2,1,0:T(8,128)(2,1)} %bitcast.8), calls=%async_computation | async-start | bytes 1966080 | tf_op jit(solution)/shard_map/all_to_all | solution.py:284
  19.1 29.1 %all-to-all-done = bf16[16,48,640]{2,1,0:T(8,128)(2,1)S(1)} async-done(((bf16[16,48,640]{2,1,0:T(8,128)(2,1)}), bf16[16,48,640]{2,1,0:T(8,128)(2,1)S(1)}, u32[]{:S(2)}, u32[]{:S(2)}) %all-to-all-start) | async-done | bytes 983072 | tf_op jit(solution)/shard_map/all_to_all | solution.py:284
  48.4 1.6 broadcast_in_dim.10
  50.0 4.6 %all-to-all-start.1 = ((bf16[4,768,384]{2,1,0:T(8,128)(2,1)}), bf16[4,768,384]{2,1,0:T(8,128)(2,1)}, u32[]{:S(2)}, u32[]{:S(2)}) async-start(bf16[4,768,384]{2,1,0:T(8,128)(2,1)} %broadcast_in_dim.10), calls=%async_computation.1 | async-start | bytes 4718592 | tf_op jit(solution)/shard_map/all_to_all | solution.py:342
  54.8 1.9 %collective-permute-start.4 = (bf16[768,256]{1,0:T(8,128)(2,1)S(1)}, bf16[768,256]{1,0:T(8,128)(2,1)S(1)}, u32[]{:S(2)}, u32[]{:S(2)}) collective-permute-start(bf16[768,256]{1,0:T(8,128)(2,1)S(1)} %pad_maximum_fusion.5), channel_id=1, source_target_pairs={{14,0},{30,16},{0,2},{16,18},{2,4},{18,20},{4,6},{20,22},{6,8},{22... | collective-permute-start | bytes 1179656 | tf_op jit(solution)/shard_map/ppermute | solution.py:276
  56.7 5.3 %collective-permute-start.3 = (bf16[768,256]{1,0:T(8,128)(2,1)S(1)}, bf16[768,256]{1,0:T(8,128)(2,1)S(1)}, u32[]{:S(2)}, u32[]{:S(2)}) collective-permute-start(bf16[768,256]{1,0:T(8,128)(2,1)S(1)} %pad_maximum_fusion.5), channel_id=1, source_target_pairs={{4,0},{28,16},{6,2},{30,18},{8,4},{16,20},{10,6},{18,22},{12,8},{2... | collective-permute-start | bytes 1179656 | tf_op jit(solution)/shard_map/ppermute | solution.py:276
  62.0 2.5 %collective-permute-start.2 = (bf16[768,256]{1,0:T(8,128)(2,1)S(1)}, bf16[768,256]{1,0:T(8,128)(2,1)S(1)}, u32[]{:S(2)}, u32[]{:S(2)}) collective-permute-start(bf16[768,256]{1,0:T(8,128)(2,1)S(1)} %pad_maximum_fusion.5), channel_id=1, source_target_pairs={{2,0},{18,16},{4,2},{20,18},{6,4},{22,20},{8,6},{24,22},{10,8},{26... | collective-permute-start | bytes 1179656 | tf_op jit(solution)/shard_map/ppermute | solution.py:276
  64.6 1.9 %collective-permute-start = (bf16[128,640]{1,0:T(8,128)(2,1)S(1)}, bf16[128,640]{1,0:T(8,128)(2,1)S(1)}, u32[]{:S(2)}, u32[]{:S(2)}) collective-permute-start(bf16[128,640]{1,0:T(8,128)(2,1)S(1)} %get-tuple-element.41), channel_id=1, source_target_pairs={{0,1},{1,2},{2,3},{3,4},{4,5},{5,6},{6,7},{7,8},{8,9},{9,10},{10,1... | collective-permute-start | bytes 491528 | tf_op jit(solution)/shard_map/ppermute | solution.py:295
  66.5 8.2 %collective-permute-start.1 = (bf16[128,640]{1,0:T(8,128)(2,1)S(1)}, bf16[128,640]{1,0:T(8,128)(2,1)S(1)}, u32[]{:S(2)}, u32[]{:S(2)}) collective-permute-start(bf16[128,640]{1,0:T(8,128)(2,1)S(1)} %get-tuple-element.42), channel_id=1, source_target_pairs={{1,0},{2,1},{3,2},{4,3},{5,4},{6,5},{7,6},{8,7},{9,8},{10,9},{11,1... | collective-permute-start | bytes 491528 | tf_op jit(solution)/shard_map/ppermute | solution.py:296
  75.2 8.4 %collective-permute-done = bf16[128,640]{1,0:T(8,128)(2,1)S(1)} collective-permute-done((bf16[128,640]{1,0:T(8,128)(2,1)S(1)}, bf16[128,640]{1,0:T(8,128)(2,1)S(1)}, u32[]{:S(2)}, u32[]{:S(2)}) %collective-permute-start) | collective-permute-done | bytes 163872 | tf_op jit(solution)/shard_map/ppermute | solution.py:295
  83.6 4.9 %collective-permute-done.1 = bf16[128,640]{1,0:T(8,128)(2,1)S(1)} collective-permute-done((bf16[128,640]{1,0:T(8,128)(2,1)S(1)}, bf16[128,640]{1,0:T(8,128)(2,1)S(1)}, u32[]{:S(2)}, u32[]{:S(2)}) %collective-permute-start.1) | collective-permute-done | bytes 163872 | tf_op jit(solution)/shard_map/ppermute | solution.py:296
  88.5 4.3 %patches.1.patch_ref = bf16[8,512,768]{2,1,0:T(8,128)(2,1)} custom-call(bf16[512,640]{1,0:T(8,128)(2,1)S(1)} %pad_maximum_fusion.1.video_ref, bf16[640,1024]{1,0:T(8,128)(2,1)S(1)} %fusion.9.spread_ref.refs_4_), custom_call_target="tpu_custom_call" | custom-call | flops 671088640 | bytes 20971520 | tf_op jit(solution)/shard_map/patches/pallas_call | solution.py:63
  92.9 2.6 %collective-permute-start.5 = (bf16[4,768,384]{2,1,0:T(8,128)(2,1)}, bf16[4,768,384]{2,1,0:T(8,128)(2,1)}, u32[]{:S(2)}, u32[]{:S(2)}) collective-permute-start(bf16[4,768,384]{2,1,0:T(8,128)(2,1)} %all-to-all-done.1.first), channel_id=1, source_target_pairs={{0,16},{16,0},{1,17},{17,1},{2,18},{18,2},{3,19},{19,3},{4,20},{20... | collective-permute-start | bytes 7077896 | tf_op jit(solution)/shard_map/ppermute | solution.py:290
  95.5 1.6 pad_maximum_fusion.second
  97.1 1.9 %collective-permute-start.6 = (bf16[4,768,256]{2,1,0:T(8,128)(2,1)S(1)}, bf16[4,768,256]{2,1,0:T(8,128)(2,1)}, u32[]{:S(2)}, u32[]{:S(2)}) collective-permute-start(bf16[4,768,256]{2,1,0:T(8,128)(2,1)S(1)} %pad_maximum_fusion.second), channel_id=1, source_target_pairs={{0,16},{16,0},{1,17},{17,1},{2,18},{18,2},{3,19},{19,3},{4,20},{20... | collective-permute-start | bytes 4718600 | tf_op jit(solution)/shard_map/ppermute | solution.py:290
  99.7 5.9 %partial.1.refs_0_ = f32[512,640]{1,0:T(8,128)S(1)} custom-call(s32[3]{0:T(128)S(1)} %pad_add_fusion.place_ref, bf16[4,768,384]{2,1,0:T(8,128)(2,1)} %all-to-all-done.1.first, bf16[4,768,256]{2,1,0:T(8,128)(2,1)S(1)} %pad_maximum_fusion.second, bf16[8,512,768]{2,1,0:T(8,128)(2,1)} %patches.1.patch_ref), custom_call_target="tpu_custom_call" | custom-call | flops 2013265920 | bytes 8388608 | tf_op jit(solution)/shard_map/partial/pallas_call | solution.py:206
  105.5 1.1 copy-done.1
  106.6 10.9 %forward.1 = (bf16[256,640]{1,0:T(8,128)(2,1)}, bf16[256,640]{1,0:T(8,128)(2,1)S(1)}, bf16[384,640]{1,0:T(8,128)(2,1)S(1)}, bf16[384,640]{1,0:T(8,128)(2,1)S(1)}) custom-call(s32[3]{0:T(128)S(1)} %pad_add_fusion.place_ref, bf16[4,768,384]{2,1,0:T(8,128)(2,1)} %collective-permute-done.5.first.other_first, ...), custom_call_target="tpu_custom_call" | custom-call | flops 4026531840 | bytes 20971520 | tf_op jit(solution)/shard_map/forward/pallas_call | solution.py:226
  117.6 2.4 %collective-permute-start.7 = (bf16[384,640]{1,0:T(8,128)(2,1)S(1)}, bf16[384,640]{1,0:T(8,128)(2,1)S(1)}, u32[]{:S(2)}, u32[]{:S(2)}) collective-permute-start(bf16[384,640]{1,0:T(8,128)(2,1)S(1)} %get-tuple-element.30), channel_id=1, source_target_pairs={{0,16},{16,0},{1,17},{17,1},{2,18},{18,2},{3,19},{19,3},{4,20},{20... | collective-permute-start | bytes 1474568 | tf_op jit(solution)/shard_map/ppermute | solution.py:290
  120.0 1.5 collective-permute-done.7
  122.3 5.9 %all-to-all-start.2 = ((bf16[16,24,640]{2,1,0:T(8,128)(2,1)}), bf16[16,24,640]{2,1,0:T(8,128)(2,1)S(1)}, u32[]{:S(2)}, u32[]{:S(2)}) async-start(bf16[16,24,640]{2,1,0:T(8,128)(2,1)} %bitcast.20), calls=%async_computation.2 | async-start | bytes 983040 | tf_op jit(solution)/shard_map/all_to_all | solution.py:284
  128.3 7.5 %collective-permute-start.9 = (bf16[128,640]{1,0:T(8,128)(2,1)S(1)}, bf16[128,640]{1,0:T(8,128)(2,1)S(1)}, u32[]{:S(2)}, u32[]{:S(2)}) collective-permute-start(bf16[128,640]{1,0:T(8,128)(2,1)S(1)} %get-tuple-element.39), channel_id=1, source_target_pairs={{1,0},{2,1},{3,2},{4,3},{5,4},{6,5},{7,6},{8,7},{9,8},{10,9},{11,1... | collective-permute-start | bytes 491528 | tf_op jit(solution)/shard_map/ppermute | solution.py:296
  135.8 1.9 %collective-permute-start.8 = (bf16[128,640]{1,0:T(8,128)(2,1)S(1)}, bf16[128,640]{1,0:T(8,128)(2,1)S(1)}, u32[]{:S(2)}, u32[]{:S(2)}) collective-permute-start(bf16[128,640]{1,0:T(8,128)(2,1)S(1)} %get-tuple-element.40), channel_id=1, source_target_pairs={{0,1},{1,2},{2,3},{3,4},{4,5},{5,6},{6,7},{7,8},{8,9},{9,10},{10,1... | collective-permute-start | bytes 491528 | tf_op jit(solution)/shard_map/ppermute | solution.py:295
  137.7 5.1 %collective-permute-done.9 = bf16[128,640]{1,0:T(8,128)(2,1)S(1)} collective-permute-done((bf16[128,640]{1,0:T(8,128)(2,1)S(1)}, bf16[128,640]{1,0:T(8,128)(2,1)S(1)}, u32[]{:S(2)}, u32[]{:S(2)}) %collective-permute-start.9) | collective-permute-done | bytes 163872 | tf_op jit(solution)/shard_map/ppermute | solution.py:296
  142.8 9.9 %collective-permute-done.8 = bf16[128,640]{1,0:T(8,128)(2,1)S(1)} collective-permute-done((bf16[128,640]{1,0:T(8,128)(2,1)S(1)}, bf16[128,640]{1,0:T(8,128)(2,1)S(1)}, u32[]{:S(2)}, u32[]{:S(2)}) %collective-permute-start.8) | collective-permute-done | bytes 163872 | tf_op jit(solution)/shard_map/ppermute | solution.py:295
  153.6 14.4 %all-to-all-start.3 = ((bf16[16,24,640]{2,1,0:T(8,128)(2,1)}), bf16[16,24,640]{2,1,0:T(8,128)(2,1)S(1)}, u32[]{:S(2)}, u32[]{:S(2)}) async-start(bf16[16,24,640]{2,1,0:T(8,128)(2,1)} %broadcast_in_dim.11), calls=%async_computation.3 | async-start | bytes 983040 | tf_op jit(solution)/shard_map/all_to_all | solution.py:367
  168.0 1.1 pad_maximum_fusion.2.refs_0_
  169.1 10.8 %backward.1 = bf16[256,640]{1,0:T(8,128)(2,1)} custom-call(s32[3]{0:T(128)S(1)} %pad_add_fusion.place_ref, bf16[4,768,384]{2,1,0:T(8,128)(2,1)} %all-to-all-done.1.first, bf16[4,768,256]{2,1,0:T(8,128)(2,1)} %copy-done, bf16[4,768,384]{2,1,0:T(8,128)(2,1)} %collective-permute-done.5.first.other_first, ...), custom_call_target="tpu_custom_call" | custom-call | flops 2013265920 | bytes 31457280 | tf_op jit(solution)/shard_map/backward/pallas_call | solution.py:251
  179.8 3.2 %all-to-all-done.3 = bf16[16,24,640]{2,1,0:T(8,128)(2,1)S(1)} async-done(((bf16[16,24,640]{2,1,0:T(8,128)(2,1)}), bf16[16,24,640]{2,1,0:T(8,128)(2,1)S(1)}, u32[]{:S(2)}, u32[]{:S(2)}) %all-to-all-start.3) | async-done | bytes 491552 | tf_op jit(solution)/shard_map/all_to_all | solution.py:367
  183.1 3.6 %collective-permute-start.10 = (f32[24,640]{1,0:T(8,128)S(1)}, f32[24,640]{1,0:T(8,128)S(1)}, u32[]{:S(2)}, u32[]{:S(2)}) collective-permute-start(f32[24,640]{1,0:T(8,128)S(1)} %convert_reduce_fusion), channel_id=1, source_target_pairs={{0,16},{16,0},{1,17},{17,1},{2,18},{18,2},{3,19},{19,3},{4,20},{20... | collective-permute-start | bytes 184328 | tf_op jit(solution)/shard_map/ppermute | solution.py:290
  (65 shorter events, 5.9 us)
Async XLA Ops:
  3.9 44.4 %all-to-all-start = ((bf16[16,48,640]{2,1,0:T(8,128)(2,1)}), bf16[16,48,640]{2,1,0:T(8,128)(2,1)S(1)}, u32[]{:S(2)}, u32[]{:S(2)}) async-start(bf16[16,48,640]{2,1,0:T(8,128)(2,1)} %bitcast.8), calls=%async_computation | async-start | bytes 1966080 | tf_op jit(solution)/shard_map/all_to_all | solution.py:284
  50.0 14.5 %copy-start.2 = (bf16[1,4,64,640]{3,2,1,0:T(8,128)(2,1)S(1)}, bf16[1,4,64,640]{3,2,1,0:T(8,128)(2,1)}, u32[]{:S(2)}) copy-start(bf16[1,4,64,640]{3,2,1,0:T(8,128)(2,1)} %param.5) | copy-start | bytes 983044
  50.0 42.9 %all-to-all-start.1 = ((bf16[4,768,384]{2,1,0:T(8,128)(2,1)}), bf16[4,768,384]{2,1,0:T(8,128)(2,1)}, u32[]{:S(2)}, u32[]{:S(2)}) async-start(bf16[4,768,384]{2,1,0:T(8,128)(2,1)} %broadcast_in_dim.10), calls=%async_computation.1 | async-start | bytes 4718592 | tf_op jit(solution)/shard_map/all_to_all | solution.py:342
  54.8 38.1 %copy-start.5 = (bf16[768,256]{1,0:T(8,128)(2,1)}, bf16[768,256]{1,0:T(8,128)(2,1)S(1)}, u32[]{:S(2)}) copy-start(bf16[768,256]{1,0:T(8,128)(2,1)S(1)} %pad_maximum_fusion.5) | copy-start | bytes 1179652
  54.8 38.1 %collective-permute-start.4 = (bf16[768,256]{1,0:T(8,128)(2,1)S(1)}, bf16[768,256]{1,0:T(8,128)(2,1)S(1)}, u32[]{:S(2)}, u32[]{:S(2)}) collective-permute-start(bf16[768,256]{1,0:T(8,128)(2,1)S(1)} %pad_maximum_fusion.5), channel_id=1, source_target_pairs={{14,0},{30,16},{0,2},{16,18},{2,4},{18,20},{4,6},{20,22},{6,8},{22... | collective-permute-start | bytes 1179656 | tf_op jit(solution)/shard_map/ppermute | solution.py:276
  56.7 36.2 %collective-permute-start.3 = (bf16[768,256]{1,0:T(8,128)(2,1)S(1)}, bf16[768,256]{1,0:T(8,128)(2,1)S(1)}, u32[]{:S(2)}, u32[]{:S(2)}) collective-permute-start(bf16[768,256]{1,0:T(8,128)(2,1)S(1)} %pad_maximum_fusion.5), channel_id=1, source_target_pairs={{4,0},{28,16},{6,2},{30,18},{8,4},{16,20},{10,6},{18,22},{12,8},{2... | collective-permute-start | bytes 1179656 | tf_op jit(solution)/shard_map/ppermute | solution.py:276
  62.0 30.9 %collective-permute-start.2 = (bf16[768,256]{1,0:T(8,128)(2,1)S(1)}, bf16[768,256]{1,0:T(8,128)(2,1)S(1)}, u32[]{:S(2)}, u32[]{:S(2)}) collective-permute-start(bf16[768,256]{1,0:T(8,128)(2,1)S(1)} %pad_maximum_fusion.5), channel_id=1, source_target_pairs={{2,0},{18,16},{4,2},{20,18},{6,4},{22,20},{8,6},{24,22},{10,8},{26... | collective-permute-start | bytes 1179656 | tf_op jit(solution)/shard_map/ppermute | solution.py:276
  64.6 19.0 %collective-permute-start = (bf16[128,640]{1,0:T(8,128)(2,1)S(1)}, bf16[128,640]{1,0:T(8,128)(2,1)S(1)}, u32[]{:S(2)}, u32[]{:S(2)}) collective-permute-start(bf16[128,640]{1,0:T(8,128)(2,1)S(1)} %get-tuple-element.41), channel_id=1, source_target_pairs={{0,1},{1,2},{2,3},{3,4},{4,5},{5,6},{6,7},{7,8},{8,9},{9,10},{10,1... | collective-permute-start | bytes 491528 | tf_op jit(solution)/shard_map/ppermute | solution.py:295
  66.5 22.0 %collective-permute-start.1 = (bf16[128,640]{1,0:T(8,128)(2,1)S(1)}, bf16[128,640]{1,0:T(8,128)(2,1)S(1)}, u32[]{:S(2)}, u32[]{:S(2)}) collective-permute-start(bf16[128,640]{1,0:T(8,128)(2,1)S(1)} %get-tuple-element.42), channel_id=1, source_target_pairs={{1,0},{2,1},{3,2},{4,3},{5,4},{6,5},{7,6},{8,7},{9,8},{10,9},{11,1... | collective-permute-start | bytes 491528 | tf_op jit(solution)/shard_map/ppermute | solution.py:296
  92.9 2.6 %copy-start.6 = (bf16[768,256]{1,0:T(8,128)(2,1)}, bf16[768,256]{1,0:T(8,128)(2,1)S(1)}, u32[]{:S(2)}) copy-start(bf16[768,256]{1,0:T(8,128)(2,1)S(1)} %collective-permute-done.4) | copy-start | bytes 1179652
  92.9 2.6 %copy-start.7 = (bf16[768,256]{1,0:T(8,128)(2,1)}, bf16[768,256]{1,0:T(8,128)(2,1)S(1)}, u32[]{:S(2)}) copy-start(bf16[768,256]{1,0:T(8,128)(2,1)S(1)} %collective-permute-done.3) | copy-start | bytes 1179652
  92.9 2.6 %copy-start.8 = (bf16[768,256]{1,0:T(8,128)(2,1)}, bf16[768,256]{1,0:T(8,128)(2,1)S(1)}, u32[]{:S(2)}) copy-start(bf16[768,256]{1,0:T(8,128)(2,1)S(1)} %collective-permute-done.2) | copy-start | bytes 1179652
  92.9 13.7 %collective-permute-start.5 = (bf16[4,768,384]{2,1,0:T(8,128)(2,1)}, bf16[4,768,384]{2,1,0:T(8,128)(2,1)}, u32[]{:S(2)}, u32[]{:S(2)}) collective-permute-start(bf16[4,768,384]{2,1,0:T(8,128)(2,1)} %all-to-all-done.1.first), channel_id=1, source_target_pairs={{0,16},{16,0},{1,17},{17,1},{2,18},{18,2},{3,19},{19,3},{4,20},{20... | collective-permute-start | bytes 7077896 | tf_op jit(solution)/shard_map/ppermute | solution.py:290
  97.1 8.4 %copy-start = (bf16[4,768,256]{2,1,0:T(8,128)(2,1)}, bf16[4,768,256]{2,1,0:T(8,128)(2,1)S(1)}, u32[]{:S(2)}) copy-start(bf16[4,768,256]{2,1,0:T(8,128)(2,1)S(1)} %pad_maximum_fusion.second) | copy-start | bytes 4718596
  97.1 9.5 %collective-permute-start.6 = (bf16[4,768,256]{2,1,0:T(8,128)(2,1)S(1)}, bf16[4,768,256]{2,1,0:T(8,128)(2,1)}, u32[]{:S(2)}, u32[]{:S(2)}) collective-permute-start(bf16[4,768,256]{2,1,0:T(8,128)(2,1)S(1)} %pad_maximum_fusion.second), channel_id=1, source_target_pairs={{0,16},{16,0},{1,17},{17,1},{2,18},{18,2},{3,19},{19,3},{4,20},{20... | collective-permute-start | bytes 4718600 | tf_op jit(solution)/shard_map/ppermute | solution.py:290
  99.6 7.0 %copy-start.3 = (bf16[1,4,64,640]{3,2,1,0:T(8,128)(2,1)S(1)}, bf16[1,4,64,640]{3,2,1,0:T(8,128)(2,1)}, u32[]{:S(2)}) copy-start(bf16[1,4,64,640]{3,2,1,0:T(8,128)(2,1)} %param.6) | copy-start | bytes 983044
  99.7 7.0 %copy-start.4 = (bf16[640,640]{1,0:T(8,128)(2,1)S(1)}, bf16[640,640]{1,0:T(8,128)(2,1)}, u32[]{:S(2)}) copy-start(bf16[640,640]{1,0:T(8,128)(2,1)} %refs_4_.1) | copy-start | bytes 2457604
  105.5 1.1 copy-start.1
  117.6 3.9 %collective-permute-start.7 = (bf16[384,640]{1,0:T(8,128)(2,1)S(1)}, bf16[384,640]{1,0:T(8,128)(2,1)S(1)}, u32[]{:S(2)}, u32[]{:S(2)}) collective-permute-start(bf16[384,640]{1,0:T(8,128)(2,1)S(1)} %get-tuple-element.30), channel_id=1, source_target_pairs={{0,16},{16,0},{1,17},{17,1},{2,18},{18,2},{3,19},{19,3},{4,20},{20... | collective-permute-start | bytes 1474568 | tf_op jit(solution)/shard_map/ppermute | solution.py:290
  122.3 30.4 %all-to-all-start.2 = ((bf16[16,24,640]{2,1,0:T(8,128)(2,1)}), bf16[16,24,640]{2,1,0:T(8,128)(2,1)S(1)}, u32[]{:S(2)}, u32[]{:S(2)}) async-start(bf16[16,24,640]{2,1,0:T(8,128)(2,1)} %bitcast.20), calls=%async_computation.2 | async-start | bytes 983040 | tf_op jit(solution)/shard_map/all_to_all | solution.py:284
  128.3 14.5 %collective-permute-start.9 = (bf16[128,640]{1,0:T(8,128)(2,1)S(1)}, bf16[128,640]{1,0:T(8,128)(2,1)S(1)}, u32[]{:S(2)}, u32[]{:S(2)}) collective-permute-start(bf16[128,640]{1,0:T(8,128)(2,1)S(1)} %get-tuple-element.39), channel_id=1, source_target_pairs={{1,0},{2,1},{3,2},{4,3},{5,4},{6,5},{7,6},{8,7},{9,8},{10,9},{11,1... | collective-permute-start | bytes 491528 | tf_op jit(solution)/shard_map/ppermute | solution.py:296
  135.8 17.0 %collective-permute-start.8 = (bf16[128,640]{1,0:T(8,128)(2,1)S(1)}, bf16[128,640]{1,0:T(8,128)(2,1)S(1)}, u32[]{:S(2)}, u32[]{:S(2)}) collective-permute-start(bf16[128,640]{1,0:T(8,128)(2,1)S(1)} %get-tuple-element.40), channel_id=1, source_target_pairs={{0,1},{1,2},{2,3},{3,4},{4,5},{5,6},{6,7},{7,8},{8,9},{9,10},{10,1... | collective-permute-start | bytes 491528 | tf_op jit(solution)/shard_map/ppermute | solution.py:295
  142.8 10.8 %copy-start.9 = (bf16[128,640]{1,0:T(8,128)(2,1)}, bf16[128,640]{1,0:T(8,128)(2,1)S(1)}, u32[]{:S(2)}) copy-start(bf16[128,640]{1,0:T(8,128)(2,1)S(1)} %collective-permute-done.9) | copy-start | bytes 491524
  152.7 0.9 copy-start.10
  153.6 29.4 %all-to-all-start.3 = ((bf16[16,24,640]{2,1,0:T(8,128)(2,1)}), bf16[16,24,640]{2,1,0:T(8,128)(2,1)S(1)}, u32[]{:S(2)}, u32[]{:S(2)}) async-start(bf16[16,24,640]{2,1,0:T(8,128)(2,1)} %broadcast_in_dim.11), calls=%async_computation.3 | async-start | bytes 983040 | tf_op jit(solution)/shard_map/all_to_all | solution.py:367
  183.1 4.5 %collective-permute-start.10 = (f32[24,640]{1,0:T(8,128)S(1)}, f32[24,640]{1,0:T(8,128)S(1)}, u32[]{:S(2)}, u32[]{:S(2)}) collective-permute-start(f32[24,640]{1,0:T(8,128)S(1)} %convert_reduce_fusion), channel_id=1, source_target_pairs={{0,16},{16,0},{1,17},{17,1},{2,18},{18,2},{3,19},{19,3},{4,20},{20... | collective-permute-start | bytes 184328 | tf_op jit(solution)/shard_map/ppermute | solution.py:290

commit v2 on v1

--- a/solution.py
+++ b/solution.py
@@ -15,7 +15,7 @@
 EXT = ROWS + 2 * HALO
 PIECE = 768
 HALF = PIECE // 2
-LEFT = 384
+LEFT = 512
 TAIL = PIECE - C
 PIECES = 8
 TM = 16
@@ -70,46 +70,50 @@
         out_specs=pl.BlockSpec((PIECES, chunk, PIECE), lambda n: (0, n, 0)),
         out_shape=jax.ShapeDtypeStruct((PIECES, EXT, PIECE), BF16),
         compiler_params=pltpu.CompilerParams(vmem_limit_bytes=VMEM),
-        cost_estimate=pl.CostEstimate(flops=2 * EXT * C * PIECES * TAIL, bytes_accessed=20 * 1024 * 1024, transcendentals=0),
+        cost_estimate=pl.CostEstimate(flops=16 * EXT * C * PIECES * TAIL, bytes_accessed=20 * 1024 * 1024, transcendentals=0),
         name="patches",
     )(video_ext, spread)
 
 
-def weight_copies(place_ref, refs, which, held, sems, index):
-    quarter, start = place_ref[0], place_ref[2]
+def weight_copies(
+    place_ref, refs, which, held, sems, index, patch_ref=None, patches=None, patch_sems=None
+):
+    own, start = place_ref[0], place_ref[2]
     first, second = refs
     copies = []
-    for n in range(4):
-        left = (start + n) % 4
-        right = (quarter + n) % 4
-        pair = (
+    for quarter in range(4):
+        from_x = (quarter - start + 4) % 4
+        from_y = (quarter - own + 4) % 4
+        slot = index(quarter, which)
+        pair = [
             pltpu.make_async_copy(
-                first.at[n], held.at[index(left, which), :, pl.ds(0, LEFT)], sems.at[2 * n]
+                first.at[from_x], held.at[slot, :, pl.ds(0, LEFT)], sems.at[2 * quarter]
             ),
             pltpu.make_async_copy(
-                second.at[n], held.at[index(right, which), :, pl.ds(LEFT, C - LEFT)], sems.at[2 * n + 1]
+                second.at[from_y], held.at[slot, :, pl.ds(LEFT, C - LEFT)], sems.at[2 * quarter + 1]
             ),
-        )
+        ]
+        if patch_ref is not None:
+            pair.append(
+                pltpu.make_async_copy(
+                    patch_ref.at[2 * quarter + which], patches.at[quarter], patch_sems.at[quarter]
+                )
+            )
         for copy in pair:
             copy.start()
-        copies += pair
+        copies.append(pair)
     return copies
 
 
-def spatial_sum(patch_ref, which, patches, patch_sems, held, copies):
-    patch_copies = []
+def spatial_sum(patches, held, copies, total):
     for quarter in range(4):
-        copy = pltpu.make_async_copy(
-            patch_ref.at[2 * quarter + which], patches.at[quarter], patch_sems.at[quarter]
-        )
-        copy.start()
-        patch_copies.append(copy)
-    for copy in copies + patch_copies:
-        copy.wait()
-    value = jnp.dot(patches[0], held[0], preferred_element_type=F32)
-    for quarter in range(1, 4):
-        value += jnp.dot(patches[quarter], held[quarter], preferred_element_type=F32)
-    return value
+        for copy in copies[quarter]:
+            copy.wait()
+        value = jnp.dot(patches[quarter], held[quarter], preferred_element_type=F32)
+        if quarter == 0:
+            total[...] = value
+        else:
+            total[...] += value
 
 
 def one_core(quarter, which):
@@ -122,17 +126,31 @@
 
 def partial_kernel(place_ref, first, second, patch_ref, out_ref, held, patches, sems, patch_sems):
     core = place_ref[1]
-    copies = weight_copies(place_ref, (first, second), core, held, sems, one_core)
-    out_ref[...] = spatial_sum(patch_ref, core, patches, patch_sems, held, copies)
+    copies = weight_copies(
+        place_ref, (first, second), core, held, sems, one_core, patch_ref, patches, patch_sems
+    )
+    spatial_sum(patches, held, copies, out_ref)
 
 
 def forward_kernel(place_ref, first, second, patch_ref, *refs):
-    partial_ref, video_ref, cot_ref, temporal_ref, proj_ref, order_ref = refs[:6]
+    given = refs[:6]
     block_ref, gg_ref, keep_ref, give_ref = refs[6:10]
-    held, patches, sems, patch_sems = refs[10:]
+    held, patches, total, sems, patch_sems, given_sems = refs[10:16]
+    local = refs[16:]
+    partial_ref, video_ref, cot_ref, temporal_ref, proj_ref, order_ref = local
     core = 1 - place_ref[1]
-    copies = weight_copies(place_ref, (first, second), core, held, sems, one_core)
-    total = spatial_sum(patch_ref, core, patches, patch_sems, held, copies) + partial_ref[...]
+    copies = weight_copies(
+        place_ref, (first, second), core, held, sems, one_core, patch_ref, patches, patch_sems
+    )
+    later = [
+        pltpu.make_async_copy(given[n], local[n], given_sems.at[n]) for n in range(len(given))
+    ]
+    for copy in later:
+        copy.start()
+    spatial_sum(patches, held, copies, total)
+    for copy in later:
+        copy.wait()
+    total = total[...] + partial_ref[...]
     spatial = total.astype(BF16)
     temporal = jnp.dot(spatial[:ROWS], temporal_ref[0], preferred_element_type=F32)
     for m in (1, 2):
@@ -174,8 +192,9 @@
     )
     grad += lax.dot_general(ext[:ROWS], temporal_ref[2], nt, preferred_element_type=F32)
     grad = grad.astype(BF16).astype(F32)
-    for copy in copies:
-        copy.wait()
+    for pair in copies:
+        for copy in pair:
+            copy.wait()
     last = shifted(grad, -TAPS[8][0], -TAPS[8][1]).astype(BF16)
     for tap in range(PIECES):
         moved = shifted(grad, -TAPS[tap][0], -TAPS[tap][1]).astype(BF16)
@@ -225,7 +244,7 @@
 def forward(place, weights, patches, summed, video, cot, temporal_weight, proj_weight, order):
     return pl.pallas_call(
         forward_kernel,
-        in_specs=[pl.BlockSpec(memory_space=pltpu.SMEM)] + [anywhere()] * 3 + [whole()] * 6,
+        in_specs=[pl.BlockSpec(memory_space=pltpu.SMEM)] + [anywhere()] * 9,
         out_specs=[whole()] * 4,
         out_shape=[
             jax.ShapeDtypeStruct((ROWS, C), BF16),
@@ -236,8 +255,16 @@
         scratch_shapes=[
             pltpu.VMEM((4, PIECE, C), BF16),
             pltpu.VMEM((4, EXT, PIECE), BF16),
+            pltpu.VMEM((EXT, C), F32),
             pltpu.SemaphoreType.DMA((8,)),
             pltpu.SemaphoreType.DMA((4,)),
+            pltpu.SemaphoreType.DMA((6,)),
+            pltpu.VMEM((EXT, C), F32),
+            pltpu.VMEM((ROWS, C), BF16),
+            pltpu.VMEM((ROWS, C), BF16),
+            pltpu.VMEM((3, C, C), BF16),
+            pltpu.VMEM((C, C), BF16),
+            pltpu.VMEM((C, PIECE), BF16),
         ],
         compiler_params=pltpu.CompilerParams(vmem_limit_bytes=VMEM),
         cost_estimate=pl.CostEstimate(
@@ -276,14 +303,8 @@
     return lax.ppermute(values, ("c", "y"), pairs)
 
 
-def paired(values):
-    groups = [
-        [(zl if zh == 0 else 3 - zl) * 16 + y * 2 + zh for y in range(8) for zh in range(2)]
-        for zl in range(4)
-    ]
-    return lax.all_to_all(
-        values, ("zl", "y", "zh"), split_axis=0, concat_axis=0, axis_index_groups=groups, tiled=True
-    )
+def over_tm(values):
+    return lax.all_to_all(values, ("y", "zh"), split_axis=0, concat_axis=0, tiled=True)
 
 
 def other_core(values):
@@ -313,7 +334,7 @@
 
 def local(video, cotangent, spatial_weight, temporal_weight, proj_weight):
     core = lax.axis_index("c")
-    x, y, zl, zh = (lax.axis_index(name) for name in ("x", "y", "zl", "zh"))
+    x, y, zl = (lax.axis_index(name) for name in ("x", "y", "zl"))
     quarter = (x + y + zl) % 4
     place = jnp.stack([quarter, core, (y + zl) % 4]).astype(jnp.int32)
 
@@ -326,10 +347,8 @@
     tail = lax.dynamic_index_in_dim(tail, core, 1, keepdims=False)
     quarters = jnp.concatenate([main, tail, jnp.zeros((4, 3, C), BF16)], axis=1)
     quarters = jnp.concatenate([quarters, quarters], axis=0)
-    low = lax.dynamic_slice_in_dim(quarters, (x + jnp.where(zh == 0, zl, 3 - zl)) % 4, 4, 0)
-    high = lax.dynamic_slice_in_dim(quarters, (x + jnp.where(zh == 0, 3 - zl, zl)) % 4, 4, 0)
-    sent = jnp.stack([low, high], axis=1)
-    sent = jnp.broadcast_to(sent[None], (2, 4, 2, 48, C)).reshape(TM, 48, C)
+    sent = lax.dynamic_slice_in_dim(quarters, (x + zl) % 4, 4, 0)
+    sent = jnp.broadcast_to(sent[None, :, None], (2, 4, 2, 48, C)).reshape(TM, 48, C)
 
     def rowed(got):
         width = got.shape[2]
@@ -337,7 +356,7 @@
             [got[:, :SHARD].reshape(C, width), got[:, SHARD:].reshape(TAIL, width)], axis=0
         )
 
-    got, shared = lax.optimization_barrier((paired(sent), rows))
+    got, shared = lax.optimization_barrier((over_tm(sent), rows))
     left, right = rowed(got[:, :, :LEFT]), rowed(got[:, :, LEFT:])
     first = lax.all_to_all(
         jnp.broadcast_to(left[None], (4, PIECE, LEFT)), "x", split_axis=0, concat_axis=0, tiled=True
@@ -357,7 +376,7 @@
 
     before, after = halos(gated_grad)
     pair = (keep.astype(F32) + other_core(give).astype(F32)).astype(BF16)
-    blocks = paired(pair.reshape(TM, 24, C))
+    blocks = over_tm(pair.reshape(TM, 24, C))
     blocks, before, after = lax.optimization_barrier((blocks, before, after))
     ext = jnp.concatenate([before, gated_grad, after], axis=0)
     video_grad = backward(place, weights + others, ext, rows, cot, temporal_weight, spread)

time: 189 us -> 184 us (0.974)
  the two profiles are of different devices: /device:TPU:25 before, /device:TPU:49 now
where the time goes in v2:
time: 184 us
  starting transfers between devices  59.8 us (32%)
  blocking collectives  43.9 us (24%)
  waiting for transfers between devices  39.6 us (22%)
  Pallas kernels  29 us (16%)
  local copies, waits for them, and re-layouts  5.98 us (3%)
  other arithmetic  4.24 us (2%)
    all_to_all x1, blocking collectives, over_tm(): lax.all_to_all(values, ('y', 'zh'), split_axis=0, concat_axis=0, tiled=True)  43.9 us
    ppermute x2, waiting for transfers between devices, halos(): after = lax.ppermute(rows[:HALO], tm, [(t + 1, t) for t in range(TM - 1)])  16.4 us
    ppermute x2, starting transfers between devices, halos(): after = lax.ppermute(rows[:HALO], tm, [(t + 1, t) for t in range(TM - 1)])  16 us
    ppermute x4, starting transfers between devices, other_core(): return lax.ppermute(values, 'c', [(0, 1), (1, 0)])  12.6 us
    pallas_call x1, Pallas kernels, backward(): pl.pallas_call(backward_kernel, in_specs=[pl.BlockSpec(memory_space=pltpu...  9.75 us
    pallas_call x1, Pallas kernels, forward(): pl.pallas_call(forward_kernel, in_specs=[pl.BlockSpec(memory_space=pltpu....  8.72 us
    ppermute x2, waiting for transfers between devices, halos(): lax.ppermute(rows[ROWS - HALO:], tm, [(t, t + 1) for t in range(TM - 1)])  8.59 us
    ppermute x3, starting transfers between devices, next_quarter(): return lax.ppermute(values, ('c', 'y'), pairs)  8.04 us
  transfers between devices with their start and end apart: 14, of which 7 were waited for; matrix products, arithmetic and copies ran while one was open for 1% of the time, Pallas kernels for 11%

profile of v2, /device:TPU:49, one launch (start us, length us, event | category | flops | bytes accessed | tf_op | source)
XLA Modules:
  0.0 183.7 jit_solution(7430103307394754445)
XLA Ops:
  1.5 1.0 slice.42
  3.1 43.9 %all_to_all.20 = bf16[16,48,640]{2,1,0:T(8,128)(2,1)S(1)} all-to-all(bf16[16,48,640]{2,1,0:T(8,128)(2,1)S(1)} %bitcast.30), channel_id=1, replica_groups=mesh['x'=4,'zl'=4,'c'=2,'y'=8,'zh'=2] {'y','zh'}, dimensions={0} | all-to-all | bytes 1966080 | tf_op jit(solution)/shard_map/all_to_all | solution.py:307
  47.1 1.9 %broadcast_in_dim.10 = bf16[4,768,512]{2,1,0:T(8,128)(2,1)} broadcast(bf16[768,512]{1,0:T(8,128)(2,1)S(1)} %pad_maximum_fusion), dimensions={1,2} | broadcast | bytes 3932160 | tf_op jit(solution)/shard_map/broadcast_in_dim | solution.py:362
  49.0 4.8 %all-to-all-start.1 = ((bf16[4,768,512]{2,1,0:T(8,128)(2,1)}), bf16[4,768,512]{2,1,0:T(8,128)(2,1)}, u32[]{:S(2)}, u32[]{:S(2)}) async-start(bf16[4,768,512]{2,1,0:T(8,128)(2,1)} %broadcast_in_dim.10), calls=%async_computation.1 | async-start | bytes 6291456 | tf_op jit(solution)/shard_map/all_to_all | solution.py:361
  54.4 2.0 %collective-permute-start = (bf16[128,640]{1,0:T(8,128)(2,1)S(1)}, bf16[128,640]{1,0:T(8,128)(2,1)S(1)}, u32[]{:S(2)}, u32[]{:S(2)}) collective-permute-start(bf16[128,640]{1,0:T(8,128)(2,1)S(1)} %get-tuple-element.39), channel_id=1, source_target_pairs={{0,1},{1,2},{2,3},{3,4},{4,5},{5,6},{6,7},{7,8},{8,9},{9,10},{10,1... | collective-permute-start | bytes 491528 | tf_op jit(solution)/shard_map/ppermute | solution.py:316
  56.5 8.1 %collective-permute-start.1 = (bf16[128,640]{1,0:T(8,128)(2,1)S(1)}, bf16[128,640]{1,0:T(8,128)(2,1)S(1)}, u32[]{:S(2)}, u32[]{:S(2)}) collective-permute-start(bf16[128,640]{1,0:T(8,128)(2,1)S(1)} %get-tuple-element.40), channel_id=1, source_target_pairs={{1,0},{2,1},{3,2},{4,3},{5,4},{6,5},{7,6},{8,7},{9,8},{10,9},{11,1... | collective-permute-start | bytes 491528 | tf_op jit(solution)/shard_map/ppermute | solution.py:317
  64.6 1.9 %collective-permute-start.4 = (bf16[768,128]{1,0:T(8,128)(2,1)S(1)}, bf16[768,128]{1,0:T(8,128)(2,1)S(1)}, u32[]{:S(2)}, u32[]{:S(2)}) collective-permute-start(bf16[768,128]{1,0:T(8,128)(2,1)S(1)} %pad_maximum_fusion.4), channel_id=1, source_target_pairs={{14,0},{30,16},{0,2},{16,18},{2,4},{18,20},{4,6},{20,22},{6,8},{22... | collective-permute-start | bytes 589832 | tf_op jit(solution)/shard_map/ppermute | solution.py:303
  66.6 4.2 %collective-permute-start.3 = (bf16[768,128]{1,0:T(8,128)(2,1)S(1)}, bf16[768,128]{1,0:T(8,128)(2,1)S(1)}, u32[]{:S(2)}, u32[]{:S(2)}) collective-permute-start(bf16[768,128]{1,0:T(8,128)(2,1)S(1)} %pad_maximum_fusion.4), channel_id=1, source_target_pairs={{4,0},{28,16},{6,2},{30,18},{8,4},{16,20},{10,6},{18,22},{12,8},{2... | collective-permute-start | bytes 589832 | tf_op jit(solution)/shard_map/ppermute | solution.py:303
  70.8 1.9 %collective-permute-start.2 = (bf16[768,128]{1,0:T(8,128)(2,1)S(1)}, bf16[768,128]{1,0:T(8,128)(2,1)S(1)}, u32[]{:S(2)}, u32[]{:S(2)}) collective-permute-start(bf16[768,128]{1,0:T(8,128)(2,1)S(1)} %pad_maximum_fusion.4), channel_id=1, source_target_pairs={{2,0},{18,16},{4,2},{20,18},{6,4},{22,20},{8,6},{24,22},{10,8},{26... | collective-permute-start | bytes 589832 | tf_op jit(solution)/shard_map/ppermute | solution.py:303
  72.7 5.3 %collective-permute-done.1 = bf16[128,640]{1,0:T(8,128)(2,1)S(1)} collective-permute-done((bf16[128,640]{1,0:T(8,128)(2,1)S(1)}, bf16[128,640]{1,0:T(8,128)(2,1)S(1)}, u32[]{:S(2)}, u32[]{:S(2)}) %collective-permute-start.1) | collective-permute-done | bytes 163872 | tf_op jit(solution)/shard_map/ppermute | solution.py:317
  78.1 4.5 %patches.1.patch_ref = bf16[8,512,768]{2,1,0:T(8,128)(2,1)} custom-call(bf16[512,640]{1,0:T(8,128)(2,1)S(1)} %pad_maximum_fusion.2.video_ref, bf16[640,1024]{1,0:T(8,128)(2,1)S(1)} %fusion.9.spread_ref.refs_4_), custom_call_target="tpu_custom_call" | custom-call | flops 5368709120 | bytes 20971520 | tf_op jit(solution)/shard_map/patches/pallas_call | solution.py:63
  82.6 7.1 %all-to-all-done.1.first = bf16[4,768,512]{2,1,0:T(8,128)(2,1)} async-done(((bf16[4,768,512]{2,1,0:T(8,128)(2,1)}), bf16[4,768,512]{2,1,0:T(8,128)(2,1)}, u32[]{:S(2)}, u32[]{:S(2)}) %all-to-all-start.1) | async-done | bytes 3145760 | tf_op jit(solution)/shard_map/all_to_all | solution.py:361
  89.7 4.6 %collective-permute-start.5 = (bf16[4,768,512]{2,1,0:T(8,128)(2,1)}, bf16[4,768,512]{2,1,0:T(8,128)(2,1)}, u32[]{:S(2)}, u32[]{:S(2)}) collective-permute-start(bf16[4,768,512]{2,1,0:T(8,128)(2,1)} %all-to-all-done.1.first), channel_id=1, source_target_pairs={{0,16},{16,0},{1,17},{17,1},{2,18},{18,2},{3,19},{19,3},{4,20},{20... | collective-permute-start | bytes 9437192 | tf_op jit(solution)/shard_map/ppermute | solution.py:311
  94.6 1.9 %collective-permute-start.6 = (bf16[4,768,128]{2,1,0:T(8,128)(2,1)S(1)}, bf16[4,768,128]{2,1,0:T(8,128)(2,1)S(1)}, u32[]{:S(2)}, u32[]{:S(2)}) collective-permute-start(bf16[4,768,128]{2,1,0:T(8,128)(2,1)S(1)} %pad_maximum_fusion.1.second), channel_id=1, source_target_pairs={{0,16},{16,0},{1,17},{17,1},{2,18},{18,2},{3,19},{19,3},{4,20},{20... | collective-permute-start | bytes 2359304 | tf_op jit(solution)/shard_map/ppermute | solution.py:311
  96.5 1.2 fusion.19.refs_5_
  97.7 6.1 %partial.1.refs_0_ = f32[512,640]{1,0:T(8,128)S(1)} custom-call(s32[3]{0:T(128)S(1)} %pad_add_fusion.place_ref, bf16[4,768,512]{2,1,0:T(8,128)(2,1)} %all-to-all-done.1.first, bf16[4,768,128]{2,1,0:T(8,128)(2,1)S(1)} %pad_maximum_fusion.1.second, bf16[8,512,768]{2,1,0:T(8,128)(2,1)} %patches.1.patch_ref), custom_call_target="tpu_custom_call" | custom-call | flops 2013265920 | bytes 8388608 | tf_op jit(solution)/shard_map/partial/pallas_call | solution.py:225
  103.8 1.0 copy-done
  104.9 8.7 %forward.1 = (bf16[256,640]{1,0:T(8,128)(2,1)}, bf16[256,640]{1,0:T(8,128)(2,1)S(1)}, bf16[384,640]{1,0:T(8,128)(2,1)S(1)}, bf16[384,640]{1,0:T(8,128)(2,1)S(1)}) custom-call(s32[3]{0:T(128)S(1)} %pad_add_fusion.place_ref, bf16[4,768,512]{2,1,0:T(8,128)(2,1)} %collective-permute-done.5.first.other_first, ...), custom_call_target="tpu_custom_call" | custom-call | flops 4026531840 | bytes 20971520 | tf_op jit(solution)/shard_map/forward/pallas_call | solution.py:245
  113.6 2.4 %collective-permute-start.7 = (bf16[384,640]{1,0:T(8,128)(2,1)S(1)}, bf16[384,640]{1,0:T(8,128)(2,1)S(1)}, u32[]{:S(2)}, u32[]{:S(2)}) collective-permute-start(bf16[384,640]{1,0:T(8,128)(2,1)S(1)} %get-tuple-element.30), channel_id=1, source_target_pairs={{0,16},{16,0},{1,17},{17,1},{2,18},{18,2},{3,19},{19,3},{4,20},{20... | collective-permute-start | bytes 1474568 | tf_op jit(solution)/shard_map/ppermute | solution.py:311
  116.0 1.5 collective-permute-done.7
  117.5 0.9 add_convert_fusion
  118.4 7.2 %all-to-all-start.2 = ((bf16[16,24,640]{2,1,0:T(8,128)(2,1)}), bf16[16,24,640]{2,1,0:T(8,128)(2,1)S(1)}, u32[]{:S(2)}, u32[]{:S(2)}) async-start(bf16[16,24,640]{2,1,0:T(8,128)(2,1)} %bitcast.18), calls=%async_computation.2 | async-start | bytes 983040 | tf_op jit(solution)/shard_map/all_to_all | solution.py:307
  125.6 7.9 %collective-permute-start.9 = (bf16[128,640]{1,0:T(8,128)(2,1)S(1)}, bf16[128,640]{1,0:T(8,128)(2,1)S(1)}, u32[]{:S(2)}, u32[]{:S(2)}) collective-permute-start(bf16[128,640]{1,0:T(8,128)(2,1)S(1)} %get-tuple-element.37), channel_id=1, source_target_pairs={{1,0},{2,1},{3,2},{4,3},{5,4},{6,5},{7,6},{8,7},{9,8},{10,9},{11,1... | collective-permute-start | bytes 491528 | tf_op jit(solution)/shard_map/ppermute | solution.py:317
  133.5 1.9 %collective-permute-start.8 = (bf16[128,640]{1,0:T(8,128)(2,1)S(1)}, bf16[128,640]{1,0:T(8,128)(2,1)S(1)}, u32[]{:S(2)}, u32[]{:S(2)}) collective-permute-start(bf16[128,640]{1,0:T(8,128)(2,1)S(1)} %get-tuple-element.38), channel_id=1, source_target_pairs={{0,1},{1,2},{2,3},{3,4},{4,5},{5,6},{6,7},{7,8},{8,9},{9,10},{10,1... | collective-permute-start | bytes 491528 | tf_op jit(solution)/shard_map/ppermute | solution.py:316
  135.5 11.0 %collective-permute-done.9 = bf16[128,640]{1,0:T(8,128)(2,1)S(1)} collective-permute-done((bf16[128,640]{1,0:T(8,128)(2,1)S(1)}, bf16[128,640]{1,0:T(8,128)(2,1)S(1)}, u32[]{:S(2)}, u32[]{:S(2)}) %collective-permute-start.9) | collective-permute-done | bytes 163872 | tf_op jit(solution)/shard_map/ppermute | solution.py:317
  146.5 8.6 %collective-permute-done.8 = bf16[128,640]{1,0:T(8,128)(2,1)S(1)} collective-permute-done((bf16[128,640]{1,0:T(8,128)(2,1)S(1)}, bf16[128,640]{1,0:T(8,128)(2,1)S(1)}, u32[]{:S(2)}, u32[]{:S(2)}) %collective-permute-start.8) | collective-permute-done | bytes 163872 | tf_op jit(solution)/shard_map/ppermute | solution.py:316
  155.2 0.8 broadcast_in_dim.11
  156.0 7.4 %all-to-all-start.3 = ((bf16[16,24,640]{2,1,0:T(8,128)(2,1)}), bf16[16,24,640]{2,1,0:T(8,128)(2,1)S(1)}, u32[]{:S(2)}, u32[]{:S(2)}) async-start(bf16[16,24,640]{2,1,0:T(8,128)(2,1)} %broadcast_in_dim.11), calls=%async_computation.3 | async-start | bytes 983040 | tf_op jit(solution)/shard_map/all_to_all | solution.py:386
  163.4 9.8 %backward.1 = bf16[256,640]{1,0:T(8,128)(2,1)} custom-call(s32[3]{0:T(128)S(1)} %pad_add_fusion.place_ref, bf16[4,768,512]{2,1,0:T(8,128)(2,1)} %all-to-all-done.1.first, bf16[4,768,128]{2,1,0:T(8,128)(2,1)S(1)} %pad_maximum_fusion.1.second, bf16[4,768,512]{2,1,0:T(8,128)(2,1)} %collective-permute-done.5.first.other_first, ...), custom_call_target="tpu_custom_call" | custom-call | flops 2013265920 | bytes 31457280 | tf_op jit(solution)/shard_map/backward/pallas_call | solution.py:278
  173.2 5.2 %all-to-all-done.3 = bf16[16,24,640]{2,1,0:T(8,128)(2,1)S(1)} async-done(((bf16[16,24,640]{2,1,0:T(8,128)(2,1)}), bf16[16,24,640]{2,1,0:T(8,128)(2,1)S(1)}, u32[]{:S(2)}, u32[]{:S(2)}) %all-to-all-start.3) | async-done | bytes 491552 | tf_op jit(solution)/shard_map/all_to_all | solution.py:386
  178.5 3.6 %collective-permute-start.10 = (f32[24,640]{1,0:T(8,128)S(1)}, f32[24,640]{1,0:T(8,128)S(1)}, u32[]{:S(2)}, u32[]{:S(2)}) collective-permute-start(f32[24,640]{1,0:T(8,128)S(1)} %convert_reduce_fusion), channel_id=1, source_target_pairs={{0,16},{16,0},{1,17},{17,1},{2,18},{18,2},{3,19},{19,3},{4,20},{20... | collective-permute-start | bytes 184328 | tf_op jit(solution)/shard_map/ppermute | solution.py:311
  182.1 0.9 collective-permute-done.10
  (50 shorter events, 3.3 us)
Async XLA Ops:
  49.0 5.4 %copy-start.2 = (bf16[1,4,64,640]{3,2,1,0:T(8,128)(2,1)S(1)}, bf16[1,4,64,640]{3,2,1,0:T(8,128)(2,1)}, u32[]{:S(2)}) copy-start(bf16[1,4,64,640]{3,2,1,0:T(8,128)(2,1)} %param.5) | copy-start | bytes 983044
  49.0 40.7 %all-to-all-start.1 = ((bf16[4,768,512]{2,1,0:T(8,128)(2,1)}), bf16[4,768,512]{2,1,0:T(8,128)(2,1)}, u32[]{:S(2)}, u32[]{:S(2)}) async-start(bf16[4,768,512]{2,1,0:T(8,128)(2,1)} %broadcast_in_dim.10), calls=%async_computation.1 | async-start | bytes 6291456 | tf_op jit(solution)/shard_map/all_to_all | solution.py:361
  54.4 28.1 %copy-start.1 = (bf16[640,1024]{1,0:T(8,128)(2,1)}, bf16[640,1024]{1,0:T(8,128)(2,1)S(1)}, u32[]{:S(2)}) copy-start(bf16[640,1024]{1,0:T(8,128)(2,1)S(1)} %fusion.9.spread_ref.refs_4_) | copy-start | bytes 3932164
  54.4 18.2 %collective-permute-start = (bf16[128,640]{1,0:T(8,128)(2,1)S(1)}, bf16[128,640]{1,0:T(8,128)(2,1)S(1)}, u32[]{:S(2)}, u32[]{:S(2)}) collective-permute-start(bf16[128,640]{1,0:T(8,128)(2,1)S(1)} %get-tuple-element.39), channel_id=1, source_target_pairs={{0,1},{1,2},{2,3},{3,4},{4,5},{5,6},{6,7},{7,8},{8,9},{9,10},{10,1... | collective-permute-start | bytes 491528 | tf_op jit(solution)/shard_map/ppermute | solution.py:316
  56.5 21.5 %collective-permute-start.1 = (bf16[128,640]{1,0:T(8,128)(2,1)S(1)}, bf16[128,640]{1,0:T(8,128)(2,1)S(1)}, u32[]{:S(2)}, u32[]{:S(2)}) collective-permute-start(bf16[128,640]{1,0:T(8,128)(2,1)S(1)} %get-tuple-element.40), channel_id=1, source_target_pairs={{1,0},{2,1},{3,2},{4,3},{5,4},{6,5},{7,6},{8,7},{9,8},{10,9},{11,1... | collective-permute-start | bytes 491528 | tf_op jit(solution)/shard_map/ppermute | solution.py:317
  64.6 17.9 %collective-permute-start.4 = (bf16[768,128]{1,0:T(8,128)(2,1)S(1)}, bf16[768,128]{1,0:T(8,128)(2,1)S(1)}, u32[]{:S(2)}, u32[]{:S(2)}) collective-permute-start(bf16[768,128]{1,0:T(8,128)(2,1)S(1)} %pad_maximum_fusion.4), channel_id=1, source_target_pairs={{14,0},{30,16},{0,2},{16,18},{2,4},{18,20},{4,6},{20,22},{6,8},{22... | collective-permute-start | bytes 589832 | tf_op jit(solution)/shard_map/ppermute | solution.py:303
  66.6 16.0 %collective-permute-start.3 = (bf16[768,128]{1,0:T(8,128)(2,1)S(1)}, bf16[768,128]{1,0:T(8,128)(2,1)S(1)}, u32[]{:S(2)}, u32[]{:S(2)}) collective-permute-start(bf16[768,128]{1,0:T(8,128)(2,1)S(1)} %pad_maximum_fusion.4), channel_id=1, source_target_pairs={{4,0},{28,16},{6,2},{30,18},{8,4},{16,20},{10,6},{18,22},{12,8},{2... | collective-permute-start | bytes 589832 | tf_op jit(solution)/shard_map/ppermute | solution.py:303
  70.8 11.8 %collective-permute-start.2 = (bf16[768,128]{1,0:T(8,128)(2,1)S(1)}, bf16[768,128]{1,0:T(8,128)(2,1)S(1)}, u32[]{:S(2)}, u32[]{:S(2)}) collective-permute-start(bf16[768,128]{1,0:T(8,128)(2,1)S(1)} %pad_maximum_fusion.4), channel_id=1, source_target_pairs={{2,0},{18,16},{4,2},{20,18},{6,4},{22,20},{8,6},{24,22},{10,8},{26... | collective-permute-start | bytes 589832 | tf_op jit(solution)/shard_map/ppermute | solution.py:303
  89.7 15.2 %collective-permute-start.5 = (bf16[4,768,512]{2,1,0:T(8,128)(2,1)}, bf16[4,768,512]{2,1,0:T(8,128)(2,1)}, u32[]{:S(2)}, u32[]{:S(2)}) collective-permute-start(bf16[4,768,512]{2,1,0:T(8,128)(2,1)} %all-to-all-done.1.first), channel_id=1, source_target_pairs={{0,16},{16,0},{1,17},{17,1},{2,18},{18,2},{3,19},{19,3},{4,20},{20... | collective-permute-start | bytes 9437192 | tf_op jit(solution)/shard_map/ppermute | solution.py:311
  94.6 10.3 %collective-permute-start.6 = (bf16[4,768,128]{2,1,0:T(8,128)(2,1)S(1)}, bf16[4,768,128]{2,1,0:T(8,128)(2,1)S(1)}, u32[]{:S(2)}, u32[]{:S(2)}) collective-permute-start(bf16[4,768,128]{2,1,0:T(8,128)(2,1)S(1)} %pad_maximum_fusion.1.second), channel_id=1, source_target_pairs={{0,16},{16,0},{1,17},{17,1},{2,18},{18,2},{3,19},{19,3},{4,20},{20... | collective-permute-start | bytes 2359304 | tf_op jit(solution)/shard_map/ppermute | solution.py:311
  97.7 7.2 %copy-start.3 = (bf16[1,4,64,640]{3,2,1,0:T(8,128)(2,1)S(1)}, bf16[1,4,64,640]{3,2,1,0:T(8,128)(2,1)}, u32[]{:S(2)}) copy-start(bf16[1,4,64,640]{3,2,1,0:T(8,128)(2,1)} %param.6) | copy-start | bytes 983044
  97.7 7.2 %copy-start.4 = (bf16[640,640]{1,0:T(8,128)(2,1)S(1)}, bf16[640,640]{1,0:T(8,128)(2,1)}, u32[]{:S(2)}) copy-start(bf16[640,640]{1,0:T(8,128)(2,1)} %refs_4_.1) | copy-start | bytes 2457604
  103.8 1.1 copy-start
  113.6 3.9 %collective-permute-start.7 = (bf16[384,640]{1,0:T(8,128)(2,1)S(1)}, bf16[384,640]{1,0:T(8,128)(2,1)S(1)}, u32[]{:S(2)}, u32[]{:S(2)}) collective-permute-start(bf16[384,640]{1,0:T(8,128)(2,1)S(1)} %get-tuple-element.30), channel_id=1, source_target_pairs={{0,16},{16,0},{1,17},{17,1},{2,18},{18,2},{3,19},{19,3},{4,20},{20... | collective-permute-start | bytes 1474568 | tf_op jit(solution)/shard_map/ppermute | solution.py:311
  118.4 36.7 %all-to-all-start.2 = ((bf16[16,24,640]{2,1,0:T(8,128)(2,1)}), bf16[16,24,640]{2,1,0:T(8,128)(2,1)S(1)}, u32[]{:S(2)}, u32[]{:S(2)}) async-start(bf16[16,24,640]{2,1,0:T(8,128)(2,1)} %bitcast.18), calls=%async_computation.2 | async-start | bytes 983040 | tf_op jit(solution)/shard_map/all_to_all | solution.py:307
  125.6 20.9 %collective-permute-start.9 = (bf16[128,640]{1,0:T(8,128)(2,1)S(1)}, bf16[128,640]{1,0:T(8,128)(2,1)S(1)}, u32[]{:S(2)}, u32[]{:S(2)}) collective-permute-start(bf16[128,640]{1,0:T(8,128)(2,1)S(1)} %get-tuple-element.37), channel_id=1, source_target_pairs={{1,0},{2,1},{3,2},{4,3},{5,4},{6,5},{7,6},{8,7},{9,8},{10,9},{11,1... | collective-permute-start | bytes 491528 | tf_op jit(solution)/shard_map/ppermute | solution.py:317
  133.5 21.6 %collective-permute-start.8 = (bf16[128,640]{1,0:T(8,128)(2,1)S(1)}, bf16[128,640]{1,0:T(8,128)(2,1)S(1)}, u32[]{:S(2)}, u32[]{:S(2)}) collective-permute-start(bf16[128,640]{1,0:T(8,128)(2,1)S(1)} %get-tuple-element.38), channel_id=1, source_target_pairs={{0,1},{1,2},{2,3},{3,4},{4,5},{5,6},{6,7},{7,8},{8,9},{9,10},{10,1... | collective-permute-start | bytes 491528 | tf_op jit(solution)/shard_map/ppermute | solution.py:316
  156.0 22.4 %all-to-all-start.3 = ((bf16[16,24,640]{2,1,0:T(8,128)(2,1)}), bf16[16,24,640]{2,1,0:T(8,128)(2,1)S(1)}, u32[]{:S(2)}, u32[]{:S(2)}) async-start(bf16[16,24,640]{2,1,0:T(8,128)(2,1)} %broadcast_in_dim.11), calls=%async_computation.3 | async-start | bytes 983040 | tf_op jit(solution)/shard_map/all_to_all | solution.py:386
  178.5 4.5 %collective-permute-start.10 = (f32[24,640]{1,0:T(8,128)S(1)}, f32[24,640]{1,0:T(8,128)S(1)}, u32[]{:S(2)}, u32[]{:S(2)}) collective-permute-start(f32[24,640]{1,0:T(8,128)S(1)} %convert_reduce_fusion), channel_id=1, source_target_pairs={{0,16},{16,0},{1,17},{17,1},{2,18},{18,2},{3,19},{19,3},{4,20},{20... | collective-permute-start | bytes 184328 | tf_op jit(solution)/shard_map/ppermute | solution.py:311

commit v3 on v2

--- a/solution.py
+++ b/solution.py
@@ -307,6 +307,16 @@
     return lax.all_to_all(values, ("y", "zh"), split_axis=0, concat_axis=0, tiled=True)
 
 
+def paired(values):
+    groups = [
+        [(zl if zh == 0 else 3 - zl) * 16 + y * 2 + zh for y in range(8) for zh in range(2)]
+        for zl in range(4)
+    ]
+    return lax.all_to_all(
+        values, ("zl", "y", "zh"), split_axis=0, concat_axis=0, axis_index_groups=groups, tiled=True
+    )
+
+
 def other_core(values):
     return lax.ppermute(values, "c", [(0, 1), (1, 0)])
 
@@ -334,7 +344,7 @@
 
 def local(video, cotangent, spatial_weight, temporal_weight, proj_weight):
     core = lax.axis_index("c")
-    x, y, zl = (lax.axis_index(name) for name in ("x", "y", "zl"))
+    x, y, zl, zh = (lax.axis_index(name) for name in ("x", "y", "zl", "zh"))
     quarter = (x + y + zl) % 4
     place = jnp.stack([quarter, core, (y + zl) % 4]).astype(jnp.int32)
 
@@ -347,8 +357,10 @@
     tail = lax.dynamic_index_in_dim(tail, core, 1, keepdims=False)
     quarters = jnp.concatenate([main, tail, jnp.zeros((4, 3, C), BF16)], axis=1)
     quarters = jnp.concatenate([quarters, quarters], axis=0)
-    sent = lax.dynamic_slice_in_dim(quarters, (x + zl) % 4, 4, 0)
-    sent = jnp.broadcast_to(sent[None, :, None], (2, 4, 2, 48, C)).reshape(TM, 48, C)
+    low = lax.dynamic_slice_in_dim(quarters, (x + jnp.where(zh == 0, zl, 3 - zl)) % 4, 4, 0)
+    high = lax.dynamic_slice_in_dim(quarters, (x + jnp.where(zh == 0, 3 - zl, zl)) % 4, 4, 0)
+    sent = jnp.stack([low, high], axis=1)
+    sent = jnp.broadcast_to(sent[None], (2, 4, 2, 48, C)).reshape(TM, 48, C)
 
     def rowed(got):
         width = got.shape[2]
@@ -356,7 +368,7 @@
             [got[:, :SHARD].reshape(C, width), got[:, SHARD:].reshape(TAIL, width)], axis=0
         )
 
-    got, shared = lax.optimization_barrier((over_tm(sent), rows))
+    got, shared = lax.optimization_barrier((paired(sent), rows))
     left, right = rowed(got[:, :, :LEFT]), rowed(got[:, :, LEFT:])
     first = lax.all_to_all(
         jnp.broadcast_to(left[None], (4, PIECE, LEFT)), "x", split_axis=0, concat_axis=0, tiled=True
@@ -365,9 +377,11 @@
     before, after = halos(shared)
     spread = spread_matrix()
     patches = prep(jnp.concatenate([before, rows, after], axis=0), spread)
-    first, patches, *second = lax.optimization_barrier((first, patches, *second))
-    weights = [first, jnp.stack(second)]
-    others = [other_core(v) for v in weights]
+    patches, *second = lax.optimization_barrier((patches, *second))
+    second = jnp.stack(second)
+    first, other_second = lax.optimization_barrier((first, other_core(second)))
+    weights = [first, second]
+    others = [other_core(first), other_second]
 
     summed = partial(place, weights, patches)
     block_out, gated_grad, keep, give = forward(

time: 184 us -> 183 us (level)
  the two profiles are of different devices: /device:TPU:49 before, /device:TPU:33 now
where the time goes in v3:
time: 183 us; the launch traced here: 182 us
  starting transfers between devices  81.3 us (44%)
  waiting for transfers between devices  59.4 us (32%)
  Pallas kernels  29 us (16%)
  local copies, waits for them, and re-layouts  7.01 us (4%)
  other arithmetic  3.99 us (2%)
    all_to_all x1, waiting for transfers between devices, paired(): lax.all_to_all(values, ('zl', 'y', 'zh'), split_axis=0, concat_axis=0, ax...  26.1 us
    ppermute x2, waiting for transfers between devices, halos(): after = lax.ppermute(rows[:HALO], tm, [(t + 1, t) for t in range(TM - 1)])  19.7 us
    ppermute x2, starting transfers between devices, halos(): after = lax.ppermute(rows[:HALO], tm, [(t + 1, t) for t in range(TM - 1)])  16.2 us
    ppermute x4, starting transfers between devices, other_core(): return lax.ppermute(values, 'c', [(0, 1), (1, 0)])  16.2 us
    all_to_all x1, starting transfers between devices, paired(): lax.all_to_all(values, ('zl', 'y', 'zh'), split_axis=0, concat_axis=0, ax...  15.1 us
    ppermute x3, starting transfers between devices, next_quarter(): return lax.ppermute(values, ('c', 'y'), pairs)  11.2 us
    pallas_call x1, Pallas kernels, backward(): pl.pallas_call(backward_kernel, in_specs=[pl.BlockSpec(memory_space=pltpu...  9.75 us
    all_to_all x1, starting transfers between devices, over_tm(): lax.all_to_all(values, ('y', 'zh'), split_axis=0, concat_axis=0, tiled=True)  8.92 us
  transfers between devices with their start and end apart: 15, of which 8 were waited for; matrix products, arithmetic and copies ran while one was open for 1% of the time, Pallas kernels for 11%

profile of v3, /device:TPU:33, one launch (start us, length us, event | category | flops | bytes accessed | tf_op | source)
XLA Modules:
  0.0 181.8 jit_solution(662790628310129850)
XLA Ops:
  1.5 1.0 slice.42
  2.8 1.1 broadcast_in_dim.9
  3.9 15.1 %all-to-all-start = ((bf16[16,48,640]{2,1,0:T(8,128)(2,1)}), bf16[16,48,640]{2,1,0:T(8,128)(2,1)S(1)}, u32[]{:S(2)}, u32[]{:S(2)}) async-start(bf16[16,48,640]{2,1,0:T(8,128)(2,1)} %bitcast.8), calls=%async_computation | async-start | bytes 1966080 | tf_op jit(solution)/shard_map/all_to_all | solution.py:315
  19.1 26.1 %all-to-all-done = bf16[16,48,640]{2,1,0:T(8,128)(2,1)S(1)} async-done(((bf16[16,48,640]{2,1,0:T(8,128)(2,1)}), bf16[16,48,640]{2,1,0:T(8,128)(2,1)S(1)}, u32[]{:S(2)}, u32[]{:S(2)}) %all-to-all-start) | async-done | bytes 983072 | tf_op jit(solution)/shard_map/all_to_all | solution.py:315
  45.3 1.9 %broadcast_in_dim.10 = bf16[4,768,512]{2,1,0:T(8,128)(2,1)} broadcast(bf16[768,512]{1,0:T(8,128)(2,1)S(1)} %pad_maximum_fusion), dimensions={1,2} | broadcast | bytes 3932160 | tf_op jit(solution)/shard_map/broadcast_in_dim | solution.py:374
  47.2 4.8 %all-to-all-start.1 = ((bf16[4,768,512]{2,1,0:T(8,128)(2,1)}), bf16[4,768,512]{2,1,0:T(8,128)(2,1)}, u32[]{:S(2)}, u32[]{:S(2)}) async-start(bf16[4,768,512]{2,1,0:T(8,128)(2,1)} %broadcast_in_dim.10), calls=%async_computation.1 | async-start | bytes 6291456 | tf_op jit(solution)/shard_map/all_to_all | solution.py:373
  52.6 2.1 %collective-permute-start = (bf16[128,640]{1,0:T(8,128)(2,1)S(1)}, bf16[128,640]{1,0:T(8,128)(2,1)S(1)}, u32[]{:S(2)}, u32[]{:S(2)}) collective-permute-start(bf16[128,640]{1,0:T(8,128)(2,1)S(1)} %get-tuple-element.43), channel_id=1, source_target_pairs={{0,1},{1,2},{2,3},{3,4},{4,5},{5,6},{6,7},{7,8},{8,9},{9,10},{10,1... | collective-permute-start | bytes 491528 | tf_op jit(solution)/shard_map/ppermute | solution.py:326
  54.7 9.2 %collective-permute-start.1 = (bf16[128,640]{1,0:T(8,128)(2,1)S(1)}, bf16[128,640]{1,0:T(8,128)(2,1)S(1)}, u32[]{:S(2)}, u32[]{:S(2)}) collective-permute-start(bf16[128,640]{1,0:T(8,128)(2,1)S(1)} %get-tuple-element.44), channel_id=1, source_target_pairs={{1,0},{2,1},{3,2},{4,3},{5,4},{6,5},{7,6},{8,7},{9,8},{10,9},{11,1... | collective-permute-start | bytes 491528 | tf_op jit(solution)/shard_map/ppermute | solution.py:327
  64.0 4.1 %collective-permute-start.4 = (bf16[768,128]{1,0:T(8,128)(2,1)S(1)}, bf16[768,128]{1,0:T(8,128)(2,1)S(1)}, u32[]{:S(2)}, u32[]{:S(2)}) collective-permute-start(bf16[768,128]{1,0:T(8,128)(2,1)S(1)} %pad_maximum_fusion.5), channel_id=1, source_target_pairs={{14,0},{30,16},{0,2},{16,18},{2,4},{18,20},{4,6},{20,22},{6,8},{22... | collective-permute-start | bytes 589832 | tf_op jit(solution)/shard_map/ppermute | solution.py:303
  68.1 2.5 %collective-permute-start.3 = (bf16[768,128]{1,0:T(8,128)(2,1)S(1)}, bf16[768,128]{1,0:T(8,128)(2,1)S(1)}, u32[]{:S(2)}, u32[]{:S(2)}) collective-permute-start(bf16[768,128]{1,0:T(8,128)(2,1)S(1)} %pad_maximum_fusion.5), channel_id=1, source_target_pairs={{4,0},{28,16},{6,2},{30,18},{8,4},{16,20},{10,6},{18,22},{12,8},{2... | collective-permute-start | bytes 589832 | tf_op jit(solution)/shard_map/ppermute | solution.py:303
  70.6 4.6 %collective-permute-start.2 = (bf16[768,128]{1,0:T(8,128)(2,1)S(1)}, bf16[768,128]{1,0:T(8,128)(2,1)S(1)}, u32[]{:S(2)}, u32[]{:S(2)}) collective-permute-start(bf16[768,128]{1,0:T(8,128)(2,1)S(1)} %pad_maximum_fusion.5), channel_id=1, source_target_pairs={{2,0},{18,16},{4,2},{20,18},{6,4},{22,20},{8,6},{24,22},{10,8},{26... | collective-permute-start | bytes 589832 | tf_op jit(solution)/shard_map/ppermute | solution.py:303
  75.4 4.4 %patches.1.patch_ref = bf16[8,512,768]{2,1,0:T(8,128)(2,1)} custom-call(bf16[512,640]{1,0:T(8,128)(2,1)S(1)} %pad_maximum_fusion.2.video_ref, bf16[640,1024]{1,0:T(8,128)(2,1)S(1)} %fusion.9.spread_ref.refs_4_), custom_call_target="tpu_custom_call" | custom-call | flops 5368709120 | bytes 20971520 | tf_op jit(solution)/shard_map/patches/pallas_call | solution.py:63
  80.0 6.4 %collective-permute-start.5 = (bf16[4,768,128]{2,1,0:T(8,128)(2,1)S(1)}, bf16[4,768,128]{2,1,0:T(8,128)(2,1)S(1)}, u32[]{:S(2)}, u32[]{:S(2)}) collective-permute-start(bf16[4,768,128]{2,1,0:T(8,128)(2,1)S(1)} %pad_maximum_fusion.1.second), channel_id=1, source_target_pairs={{0,16},{16,0},{1,17},{17,1},{2,18},{18,2},{3,19},{19,3},{4,20},{20... | collective-permute-start | bytes 2359304 | tf_op jit(solution)/shard_map/ppermute | solution.py:321
  86.4 1.9 %collective-permute-done.5.second.other_second = bf16[4,768,128]{2,1,0:T(8,128)(2,1)S(1)} collective-permute-done((bf16[4,768,128]{2,1,0:T(8,128)(2,1)S(1)}, bf16[4,768,128]{2,1,0:T(8,128)(2,1)S(1)}, u32[]{:S(2)}, u32[]{:S(2)}) %collective-permute-start.5) | collective-permute-done | bytes 786464 | tf_op jit(solution)/shard_map/ppermute | solution.py:321
  88.3 4.2 %collective-permute-start.6 = (bf16[4,768,512]{2,1,0:T(8,128)(2,1)}, bf16[4,768,512]{2,1,0:T(8,128)(2,1)}, u32[]{:S(2)}, u32[]{:S(2)}) collective-permute-start(bf16[4,768,512]{2,1,0:T(8,128)(2,1)} %all-to-all-done.1.first), channel_id=1, source_target_pairs={{0,16},{16,0},{1,17},{17,1},{2,18},{18,2},{3,19},{19,3},{4,20},{20... | collective-permute-start | bytes 9437192 | tf_op jit(solution)/shard_map/ppermute | solution.py:321
  92.6 1.2 fusion.19.refs_5_
  93.9 6.1 %partial.1.refs_0_ = f32[512,640]{1,0:T(8,128)S(1)} custom-call(s32[3]{0:T(128)S(1)} %pad_add_fusion.place_ref, bf16[4,768,512]{2,1,0:T(8,128)(2,1)} %all-to-all-done.1.first, bf16[4,768,128]{2,1,0:T(8,128)(2,1)S(1)} %pad_maximum_fusion.1.second, bf16[8,512,768]{2,1,0:T(8,128)(2,1)} %patches.1.patch_ref), custom_call_target="tpu_custom_call" | custom-call | flops 2013265920 | bytes 8388608 | tf_op jit(solution)/shard_map/partial/pallas_call | solution.py:225
  100.0 1.0 copy-done
  101.0 8.7 %forward.1 = (bf16[256,640]{1,0:T(8,128)(2,1)}, bf16[256,640]{1,0:T(8,128)(2,1)S(1)}, bf16[384,640]{1,0:T(8,128)(2,1)S(1)}, bf16[384,640]{1,0:T(8,128)(2,1)S(1)}) custom-call(s32[3]{0:T(128)S(1)} %pad_add_fusion.place_ref, bf16[4,768,512]{2,1,0:T(8,128)(2,1)} %collective-permute-done.6.first.other_first, ...), custom_call_target="tpu_custom_call" | custom-call | flops 4026531840 | bytes 20971520 | tf_op jit(solution)/shard_map/forward/pallas_call | solution.py:245
  109.8 1.9 %collective-permute-start.7 = (bf16[384,640]{1,0:T(8,128)(2,1)S(1)}, bf16[384,640]{1,0:T(8,128)(2,1)S(1)}, u32[]{:S(2)}, u32[]{:S(2)}) collective-permute-start(bf16[384,640]{1,0:T(8,128)(2,1)S(1)} %get-tuple-element.32), channel_id=1, source_target_pairs={{0,16},{16,0},{1,17},{17,1},{2,18},{18,2},{3,19},{19,3},{4,20},{20... | collective-permute-start | bytes 1474568 | tf_op jit(solution)/shard_map/ppermute | solution.py:321
  111.7 1.8 %collective-permute-done.7 = bf16[384,640]{1,0:T(8,128)(2,1)S(1)} collective-permute-done((bf16[384,640]{1,0:T(8,128)(2,1)S(1)}, bf16[384,640]{1,0:T(8,128)(2,1)S(1)}, u32[]{:S(2)}, u32[]{:S(2)}) %collective-permute-start.7) | collective-permute-done | bytes 491552 | tf_op jit(solution)/shard_map/ppermute | solution.py:321
  113.5 0.9 add_convert_fusion
  114.4 8.9 %all-to-all-start.2 = ((bf16[16,24,640]{2,1,0:T(8,128)(2,1)}), bf16[16,24,640]{2,1,0:T(8,128)(2,1)S(1)}, u32[]{:S(2)}, u32[]{:S(2)}) async-start(bf16[16,24,640]{2,1,0:T(8,128)(2,1)} %bitcast.20), calls=%async_computation.2 | async-start | bytes 983040 | tf_op jit(solution)/shard_map/all_to_all | solution.py:307
  123.4 7.0 %collective-permute-start.9 = (bf16[128,640]{1,0:T(8,128)(2,1)S(1)}, bf16[128,640]{1,0:T(8,128)(2,1)S(1)}, u32[]{:S(2)}, u32[]{:S(2)}) collective-permute-start(bf16[128,640]{1,0:T(8,128)(2,1)S(1)} %get-tuple-element.41), channel_id=1, source_target_pairs={{1,0},{2,1},{3,2},{4,3},{5,4},{6,5},{7,6},{8,7},{9,8},{10,9},{11,1... | collective-permute-start | bytes 491528 | tf_op jit(solution)/shard_map/ppermute | solution.py:327
  130.4 2.2 %collective-permute-start.8 = (bf16[128,640]{1,0:T(8,128)(2,1)S(1)}, bf16[128,640]{1,0:T(8,128)(2,1)S(1)}, u32[]{:S(2)}, u32[]{:S(2)}) collective-permute-start(bf16[128,640]{1,0:T(8,128)(2,1)S(1)} %get-tuple-element.42), channel_id=1, source_target_pairs={{0,1},{1,2},{2,3},{3,4},{4,5},{5,6},{6,7},{7,8},{8,9},{9,10},{10,1... | collective-permute-start | bytes 491528 | tf_op jit(solution)/shard_map/ppermute | solution.py:326
  132.6 19.5 %collective-permute-done.9 = bf16[128,640]{1,0:T(8,128)(2,1)S(1)} collective-permute-done((bf16[128,640]{1,0:T(8,128)(2,1)S(1)}, bf16[128,640]{1,0:T(8,128)(2,1)S(1)}, u32[]{:S(2)}, u32[]{:S(2)}) %collective-permute-start.9) | collective-permute-done | bytes 163872 | tf_op jit(solution)/shard_map/ppermute | solution.py:327
  152.1 3.9 %collective-permute-done.8 = bf16[128,640]{1,0:T(8,128)(2,1)S(1)} collective-permute-done((bf16[128,640]{1,0:T(8,128)(2,1)S(1)}, bf16[128,640]{1,0:T(8,128)(2,1)S(1)}, u32[]{:S(2)}, u32[]{:S(2)}) %collective-permute-start.8) | collective-permute-done | bytes 163872 | tf_op jit(solution)/shard_map/ppermute | solution.py:326
  156.9 4.6 %all-to-all-start.3 = ((bf16[16,24,640]{2,1,0:T(8,128)(2,1)}), bf16[16,24,640]{2,1,0:T(8,128)(2,1)S(1)}, u32[]{:S(2)}, u32[]{:S(2)}) async-start(bf16[16,24,640]{2,1,0:T(8,128)(2,1)} %broadcast_in_dim.11), calls=%async_computation.3 | async-start | bytes 983040 | tf_op jit(solution)/shard_map/all_to_all | solution.py:400
  161.6 9.8 %backward.1 = bf16[256,640]{1,0:T(8,128)(2,1)} custom-call(s32[3]{0:T(128)S(1)} %pad_add_fusion.place_ref, bf16[4,768,512]{2,1,0:T(8,128)(2,1)} %all-to-all-done.1.first, bf16[4,768,128]{2,1,0:T(8,128)(2,1)S(1)} %pad_maximum_fusion.1.second, bf16[4,768,512]{2,1,0:T(8,128)(2,1)} %collective-permute-done.6.first.other_first, ...), custom_call_target="tpu_custom_call" | custom-call | flops 2013265920 | bytes 31457280 | tf_op jit(solution)/shard_map/backward/pallas_call | solution.py:278
  171.3 5.2 %all-to-all-done.3 = bf16[16,24,640]{2,1,0:T(8,128)(2,1)S(1)} async-done(((bf16[16,24,640]{2,1,0:T(8,128)(2,1)}), bf16[16,24,640]{2,1,0:T(8,128)(2,1)S(1)}, u32[]{:S(2)}, u32[]{:S(2)}) %all-to-all-start.3) | async-done | bytes 491552 | tf_op jit(solution)/shard_map/all_to_all | solution.py:400
  176.6 3.6 %collective-permute-start.10 = (f32[24,640]{1,0:T(8,128)S(1)}, f32[24,640]{1,0:T(8,128)S(1)}, u32[]{:S(2)}, u32[]{:S(2)}) collective-permute-start(f32[24,640]{1,0:T(8,128)S(1)} %convert_reduce_fusion), channel_id=1, source_target_pairs={{0,16},{16,0},{1,17},{17,1},{2,18},{18,2},{3,19},{19,3},{4,20},{20... | collective-permute-start | bytes 184328 | tf_op jit(solution)/shard_map/ppermute | solution.py:321
  180.3 0.9 collective-permute-done.10
  (53 shorter events, 4.0 us)
Async XLA Ops:
  3.9 41.3 %all-to-all-start = ((bf16[16,48,640]{2,1,0:T(8,128)(2,1)}), bf16[16,48,640]{2,1,0:T(8,128)(2,1)S(1)}, u32[]{:S(2)}, u32[]{:S(2)}) async-start(bf16[16,48,640]{2,1,0:T(8,128)(2,1)} %bitcast.8), calls=%async_computation | async-start | bytes 1966080 | tf_op jit(solution)/shard_map/all_to_all | solution.py:315
  47.2 5.3 %copy-start.2 = (bf16[1,4,64,640]{3,2,1,0:T(8,128)(2,1)S(1)}, bf16[1,4,64,640]{3,2,1,0:T(8,128)(2,1)}, u32[]{:S(2)}) copy-start(bf16[1,4,64,640]{3,2,1,0:T(8,128)(2,1)} %param.5) | copy-start | bytes 983044
  47.2 41.1 %all-to-all-start.1 = ((bf16[4,768,512]{2,1,0:T(8,128)(2,1)}), bf16[4,768,512]{2,1,0:T(8,128)(2,1)}, u32[]{:S(2)}, u32[]{:S(2)}) async-start(bf16[4,768,512]{2,1,0:T(8,128)(2,1)} %broadcast_in_dim.10), calls=%async_computation.1 | async-start | bytes 6291456 | tf_op jit(solution)/shard_map/all_to_all | solution.py:373
  52.5 27.3 %copy-start.1 = (bf16[640,1024]{1,0:T(8,128)(2,1)}, bf16[640,1024]{1,0:T(8,128)(2,1)S(1)}, u32[]{:S(2)}) copy-start(bf16[640,1024]{1,0:T(8,128)(2,1)S(1)} %fusion.9.spread_ref.refs_4_) | copy-start | bytes 3932164
  52.6 22.7 %collective-permute-start = (bf16[128,640]{1,0:T(8,128)(2,1)S(1)}, bf16[128,640]{1,0:T(8,128)(2,1)S(1)}, u32[]{:S(2)}, u32[]{:S(2)}) collective-permute-start(bf16[128,640]{1,0:T(8,128)(2,1)S(1)} %get-tuple-element.43), channel_id=1, source_target_pairs={{0,1},{1,2},{2,3},{3,4},{4,5},{5,6},{6,7},{7,8},{8,9},{9,10},{10,1... | collective-permute-start | bytes 491528 | tf_op jit(solution)/shard_map/ppermute | solution.py:326
  54.7 20.7 %collective-permute-start.1 = (bf16[128,640]{1,0:T(8,128)(2,1)S(1)}, bf16[128,640]{1,0:T(8,128)(2,1)S(1)}, u32[]{:S(2)}, u32[]{:S(2)}) collective-permute-start(bf16[128,640]{1,0:T(8,128)(2,1)S(1)} %get-tuple-element.44), channel_id=1, source_target_pairs={{1,0},{2,1},{3,2},{4,3},{5,4},{6,5},{7,6},{8,7},{9,8},{10,9},{11,1... | collective-permute-start | bytes 491528 | tf_op jit(solution)/shard_map/ppermute | solution.py:327
  64.0 15.9 %collective-permute-start.4 = (bf16[768,128]{1,0:T(8,128)(2,1)S(1)}, bf16[768,128]{1,0:T(8,128)(2,1)S(1)}, u32[]{:S(2)}, u32[]{:S(2)}) collective-permute-start(bf16[768,128]{1,0:T(8,128)(2,1)S(1)} %pad_maximum_fusion.5), channel_id=1, source_target_pairs={{14,0},{30,16},{0,2},{16,18},{2,4},{18,20},{4,6},{20,22},{6,8},{22... | collective-permute-start | bytes 589832 | tf_op jit(solution)/shard_map/ppermute | solution.py:303
  68.1 11.7 %collective-permute-start.3 = (bf16[768,128]{1,0:T(8,128)(2,1)S(1)}, bf16[768,128]{1,0:T(8,128)(2,1)S(1)}, u32[]{:S(2)}, u32[]{:S(2)}) collective-permute-start(bf16[768,128]{1,0:T(8,128)(2,1)S(1)} %pad_maximum_fusion.5), channel_id=1, source_target_pairs={{4,0},{28,16},{6,2},{30,18},{8,4},{16,20},{10,6},{18,22},{12,8},{2... | collective-permute-start | bytes 589832 | tf_op jit(solution)/shard_map/ppermute | solution.py:303
  70.6 9.2 %collective-permute-start.2 = (bf16[768,128]{1,0:T(8,128)(2,1)S(1)}, bf16[768,128]{1,0:T(8,128)(2,1)S(1)}, u32[]{:S(2)}, u32[]{:S(2)}) collective-permute-start(bf16[768,128]{1,0:T(8,128)(2,1)S(1)} %pad_maximum_fusion.5), channel_id=1, source_target_pairs={{2,0},{18,16},{4,2},{20,18},{6,4},{22,20},{8,6},{24,22},{10,8},{26... | collective-permute-start | bytes 589832 | tf_op jit(solution)/shard_map/ppermute | solution.py:303
  80.0 8.3 %collective-permute-start.5 = (bf16[4,768,128]{2,1,0:T(8,128)(2,1)S(1)}, bf16[4,768,128]{2,1,0:T(8,128)(2,1)S(1)}, u32[]{:S(2)}, u32[]{:S(2)}) collective-permute-start(bf16[4,768,128]{2,1,0:T(8,128)(2,1)S(1)} %pad_maximum_fusion.1.second), channel_id=1, source_target_pairs={{0,16},{16,0},{1,17},{17,1},{2,18},{18,2},{3,19},{19,3},{4,20},{20... | collective-permute-start | bytes 2359304 | tf_op jit(solution)/shard_map/ppermute | solution.py:321
  88.3 12.7 %collective-permute-start.6 = (bf16[4,768,512]{2,1,0:T(8,128)(2,1)}, bf16[4,768,512]{2,1,0:T(8,128)(2,1)}, u32[]{:S(2)}, u32[]{:S(2)}) collective-permute-start(bf16[4,768,512]{2,1,0:T(8,128)(2,1)} %all-to-all-done.1.first), channel_id=1, source_target_pairs={{0,16},{16,0},{1,17},{17,1},{2,18},{18,2},{3,19},{19,3},{4,20},{20... | collective-permute-start | bytes 9437192 | tf_op jit(solution)/shard_map/ppermute | solution.py:321
  93.9 7.2 %copy-start.3 = (bf16[1,4,64,640]{3,2,1,0:T(8,128)(2,1)S(1)}, bf16[1,4,64,640]{3,2,1,0:T(8,128)(2,1)}, u32[]{:S(2)}) copy-start(bf16[1,4,64,640]{3,2,1,0:T(8,128)(2,1)} %param.6) | copy-start | bytes 983044
  93.9 7.2 %copy-start.4 = (bf16[640,640]{1,0:T(8,128)(2,1)S(1)}, bf16[640,640]{1,0:T(8,128)(2,1)}, u32[]{:S(2)}) copy-start(bf16[640,640]{1,0:T(8,128)(2,1)} %refs_4_.1) | copy-start | bytes 2457604
  100.0 1.1 copy-start
  109.8 3.8 %collective-permute-start.7 = (bf16[384,640]{1,0:T(8,128)(2,1)S(1)}, bf16[384,640]{1,0:T(8,128)(2,1)S(1)}, u32[]{:S(2)}, u32[]{:S(2)}) collective-permute-start(bf16[384,640]{1,0:T(8,128)(2,1)S(1)} %get-tuple-element.32), channel_id=1, source_target_pairs={{0,16},{16,0},{1,17},{17,1},{2,18},{18,2},{3,19},{19,3},{4,20},{20... | collective-permute-start | bytes 1474568 | tf_op jit(solution)/shard_map/ppermute | solution.py:321
  114.4 41.6 %all-to-all-start.2 = ((bf16[16,24,640]{2,1,0:T(8,128)(2,1)}), bf16[16,24,640]{2,1,0:T(8,128)(2,1)S(1)}, u32[]{:S(2)}, u32[]{:S(2)}) async-start(bf16[16,24,640]{2,1,0:T(8,128)(2,1)} %bitcast.20), calls=%async_computation.2 | async-start | bytes 983040 | tf_op jit(solution)/shard_map/all_to_all | solution.py:307
  123.4 28.7 %collective-permute-start.9 = (bf16[128,640]{1,0:T(8,128)(2,1)S(1)}, bf16[128,640]{1,0:T(8,128)(2,1)S(1)}, u32[]{:S(2)}, u32[]{:S(2)}) collective-permute-start(bf16[128,640]{1,0:T(8,128)(2,1)S(1)} %get-tuple-element.41), channel_id=1, source_target_pairs={{1,0},{2,1},{3,2},{4,3},{5,4},{6,5},{7,6},{8,7},{9,8},{10,9},{11,1... | collective-permute-start | bytes 491528 | tf_op jit(solution)/shard_map/ppermute | solution.py:327
  130.4 25.6 %collective-permute-start.8 = (bf16[128,640]{1,0:T(8,128)(2,1)S(1)}, bf16[128,640]{1,0:T(8,128)(2,1)S(1)}, u32[]{:S(2)}, u32[]{:S(2)}) collective-permute-start(bf16[128,640]{1,0:T(8,128)(2,1)S(1)} %get-tuple-element.42), channel_id=1, source_target_pairs={{0,1},{1,2},{2,3},{3,4},{4,5},{5,6},{6,7},{7,8},{8,9},{9,10},{10,1... | collective-permute-start | bytes 491528 | tf_op jit(solution)/shard_map/ppermute | solution.py:326
  156.9 19.6 %all-to-all-start.3 = ((bf16[16,24,640]{2,1,0:T(8,128)(2,1)}), bf16[16,24,640]{2,1,0:T(8,128)(2,1)S(1)}, u32[]{:S(2)}, u32[]{:S(2)}) async-start(bf16[16,24,640]{2,1,0:T(8,128)(2,1)} %broadcast_in_dim.11), calls=%async_computation.3 | async-start | bytes 983040 | tf_op jit(solution)/shard_map/all_to_all | solution.py:400
  176.6 4.5 %collective-permute-start.10 = (f32[24,640]{1,0:T(8,128)S(1)}, f32[24,640]{1,0:T(8,128)S(1)}, u32[]{:S(2)}, u32[]{:S(2)}) collective-permute-start(f32[24,640]{1,0:T(8,128)S(1)} %convert_reduce_fusion), channel_id=1, source_target_pairs={{0,16},{16,0},{1,17},{17,1},{2,18},{18,2},{3,19},{19,3},{4,20},{20... | collective-permute-start | bytes 184328 | tf_op jit(solution)/shard_map/ppermute | solution.py:321

commit v4 on v3

--- a/solution.py
+++ b/solution.py
@@ -303,10 +303,6 @@
     return lax.ppermute(values, ("c", "y"), pairs)
 
 
-def over_tm(values):
-    return lax.all_to_all(values, ("y", "zh"), split_axis=0, concat_axis=0, tiled=True)
-
-
 def paired(values):
     groups = [
         [(zl if zh == 0 else 3 - zl) * 16 + y * 2 + zh for y in range(8) for zh in range(2)]
@@ -390,7 +386,7 @@
 
     before, after = halos(gated_grad)
     pair = (keep.astype(F32) + other_core(give).astype(F32)).astype(BF16)
-    blocks = over_tm(pair.reshape(TM, 24, C))
+    blocks = paired(pair.reshape(TM, 24, C))
     blocks, before, after = lax.optimization_barrier((blocks, before, after))
     ext = jnp.concatenate([before, gated_grad, after], axis=0)
     video_grad = backward(place, weights + others, ext, rows, cot, temporal_weight, spread)

time: 183 us -> 181 us (0.989)
  the two profiles are of different devices: /device:TPU:33 before, /device:TPU:49 now
where the time goes in v4:
time: 181 us; the launch traced here: 180 us
  starting transfers between devices  75 us (41%)
  waiting for transfers between devices  64.1 us (35%)
  Pallas kernels  28.9 us (16%)
  local copies, waits for them, and re-layouts  7.01 us (4%)
  other arithmetic  3.99 us (2%)
    all_to_all x2, waiting for transfers between devices, paired(): lax.all_to_all(values, ('zl', 'y', 'zh'), split_axis=0, concat_axis=0, ax...  29.8 us
    all_to_all x2, starting transfers between devices, paired(): lax.all_to_all(values, ('zl', 'y', 'zh'), split_axis=0, concat_axis=0, ax...  20.1 us
    ppermute x2, waiting for transfers between devices, halos(): after = lax.ppermute(rows[:HALO], tm, [(t + 1, t) for t in range(TM - 1)])  13.3 us
    ppermute x2, starting transfers between devices, halos(): after = lax.ppermute(rows[:HALO], tm, [(t + 1, t) for t in range(TM - 1)])  13.1 us
    ppermute x4, starting transfers between devices, other_core(): return lax.ppermute(values, 'c', [(0, 1), (1, 0)])  12 us
    all_to_all x1, starting transfers between devices, local(): lax.all_to_all(sent, ('x', 'zl'), split_axis=0, concat_axis=0, tiled=True)  11.7 us
    pallas_call x1, Pallas kernels, backward(): pl.pallas_call(backward_kernel, in_specs=[pl.BlockSpec(memory_space=pltpu...  9.75 us
    pallas_call x1, Pallas kernels, forward(): pl.pallas_call(forward_kernel, in_specs=[pl.BlockSpec(memory_space=pltpu....  8.73 us
  transfers between devices with their start and end apart: 15, of which 9 were waited for; matrix products, arithmetic and copies ran while one was open for 1% of the time, Pallas kernels for 11%

profile of v4, /device:TPU:49, one launch (start us, length us, event | category | flops | bytes accessed | tf_op | source)
XLA Modules:
  0.0 180.1 jit_solution(5380108692913429999)
XLA Ops:
  1.5 1.0 slice.42
  2.8 1.1 broadcast_in_dim.9
  3.9 14.9 %all-to-all-start = ((bf16[16,48,640]{2,1,0:T(8,128)(2,1)}), bf16[16,48,640]{2,1,0:T(8,128)(2,1)S(1)}, u32[]{:S(2)}, u32[]{:S(2)}) async-start(bf16[16,48,640]{2,1,0:T(8,128)(2,1)} %bitcast.8), calls=%async_computation | async-start | bytes 1966080 | tf_op jit(solution)/shard_map/all_to_all | solution.py:311
  18.8 29.8 %all-to-all-done = bf16[16,48,640]{2,1,0:T(8,128)(2,1)S(1)} async-done(((bf16[16,48,640]{2,1,0:T(8,128)(2,1)}), bf16[16,48,640]{2,1,0:T(8,128)(2,1)S(1)}, u32[]{:S(2)}, u32[]{:S(2)}) %all-to-all-start) | async-done | bytes 983072 | tf_op jit(solution)/shard_map/all_to_all | solution.py:311
  48.8 1.9 %broadcast_in_dim.10 = bf16[4,768,512]{2,1,0:T(8,128)(2,1)} broadcast(bf16[768,512]{1,0:T(8,128)(2,1)S(1)} %pad_maximum_fusion), dimensions={1,2} | broadcast | bytes 3932160 | tf_op jit(solution)/shard_map/broadcast_in_dim | solution.py:370
  50.7 4.8 %all-to-all-start.1 = ((bf16[4,768,512]{2,1,0:T(8,128)(2,1)}), bf16[4,768,512]{2,1,0:T(8,128)(2,1)}, u32[]{:S(2)}, u32[]{:S(2)}) async-start(bf16[4,768,512]{2,1,0:T(8,128)(2,1)} %broadcast_in_dim.10), calls=%async_computation.1 | async-start | bytes 6291456 | tf_op jit(solution)/shard_map/all_to_all | solution.py:369
  56.1 1.9 %collective-permute-start = (bf16[128,640]{1,0:T(8,128)(2,1)S(1)}, bf16[128,640]{1,0:T(8,128)(2,1)S(1)}, u32[]{:S(2)}, u32[]{:S(2)}) collective-permute-start(bf16[128,640]{1,0:T(8,128)(2,1)S(1)} %get-tuple-element.43), channel_id=1, source_target_pairs={{0,1},{1,2},{2,3},{3,4},{4,5},{5,6},{6,7},{7,8},{8,9},{9,10},{10,1... | collective-permute-start | bytes 491528 | tf_op jit(solution)/shard_map/ppermute | solution.py:322
  58.0 8.2 %collective-permute-start.1 = (bf16[128,640]{1,0:T(8,128)(2,1)S(1)}, bf16[128,640]{1,0:T(8,128)(2,1)S(1)}, u32[]{:S(2)}, u32[]{:S(2)}) collective-permute-start(bf16[128,640]{1,0:T(8,128)(2,1)S(1)} %get-tuple-element.44), channel_id=1, source_target_pairs={{1,0},{2,1},{3,2},{4,3},{5,4},{6,5},{7,6},{8,7},{9,8},{10,9},{11,1... | collective-permute-start | bytes 491528 | tf_op jit(solution)/shard_map/ppermute | solution.py:323
  66.3 1.9 %collective-permute-start.4 = (bf16[768,128]{1,0:T(8,128)(2,1)S(1)}, bf16[768,128]{1,0:T(8,128)(2,1)S(1)}, u32[]{:S(2)}, u32[]{:S(2)}) collective-permute-start(bf16[768,128]{1,0:T(8,128)(2,1)S(1)} %pad_maximum_fusion.5), channel_id=1, source_target_pairs={{14,0},{30,16},{0,2},{16,18},{2,4},{18,20},{4,6},{20,22},{6,8},{22... | collective-permute-start | bytes 589832 | tf_op jit(solution)/shard_map/ppermute | solution.py:303
  68.2 2.8 %collective-permute-start.3 = (bf16[768,128]{1,0:T(8,128)(2,1)S(1)}, bf16[768,128]{1,0:T(8,128)(2,1)S(1)}, u32[]{:S(2)}, u32[]{:S(2)}) collective-permute-start(bf16[768,128]{1,0:T(8,128)(2,1)S(1)} %pad_maximum_fusion.5), channel_id=1, source_target_pairs={{4,0},{28,16},{6,2},{30,18},{8,4},{16,20},{10,6},{18,22},{12,8},{2... | collective-permute-start | bytes 589832 | tf_op jit(solution)/shard_map/ppermute | solution.py:303
  71.0 2.5 %collective-permute-start.2 = (bf16[768,128]{1,0:T(8,128)(2,1)S(1)}, bf16[768,128]{1,0:T(8,128)(2,1)S(1)}, u32[]{:S(2)}, u32[]{:S(2)}) collective-permute-start(bf16[768,128]{1,0:T(8,128)(2,1)S(1)} %pad_maximum_fusion.5), channel_id=1, source_target_pairs={{2,0},{18,16},{4,2},{20,18},{6,4},{22,20},{8,6},{24,22},{10,8},{26... | collective-permute-start | bytes 589832 | tf_op jit(solution)/shard_map/ppermute | solution.py:303
  73.5 6.9 %collective-permute-done.1 = bf16[128,640]{1,0:T(8,128)(2,1)S(1)} collective-permute-done((bf16[128,640]{1,0:T(8,128)(2,1)S(1)}, bf16[128,640]{1,0:T(8,128)(2,1)S(1)}, u32[]{:S(2)}, u32[]{:S(2)}) %collective-permute-start.1) | collective-permute-done | bytes 163872 | tf_op jit(solution)/shard_map/ppermute | solution.py:323
  80.4 4.4 %patches.1.patch_ref = bf16[8,512,768]{2,1,0:T(8,128)(2,1)} custom-call(bf16[512,640]{1,0:T(8,128)(2,1)S(1)} %pad_maximum_fusion.2.video_ref, bf16[640,1024]{1,0:T(8,128)(2,1)S(1)} %fusion.9.spread_ref.refs_4_), custom_call_target="tpu_custom_call" | custom-call | flops 5368709120 | bytes 20971520 | tf_op jit(solution)/shard_map/patches/pallas_call | solution.py:63
  85.0 2.7 %collective-permute-start.5 = (bf16[4,768,128]{2,1,0:T(8,128)(2,1)S(1)}, bf16[4,768,128]{2,1,0:T(8,128)(2,1)S(1)}, u32[]{:S(2)}, u32[]{:S(2)}) collective-permute-start(bf16[4,768,128]{2,1,0:T(8,128)(2,1)S(1)} %pad_maximum_fusion.1.second), channel_id=1, source_target_pairs={{0,16},{16,0},{1,17},{17,1},{2,18},{18,2},{3,19},{19,3},{4,20},{20... | collective-permute-start | bytes 2359304 | tf_op jit(solution)/shard_map/ppermute | solution.py:317
  87.7 1.9 %collective-permute-done.5.second.other_second = bf16[4,768,128]{2,1,0:T(8,128)(2,1)S(1)} collective-permute-done((bf16[4,768,128]{2,1,0:T(8,128)(2,1)S(1)}, bf16[4,768,128]{2,1,0:T(8,128)(2,1)S(1)}, u32[]{:S(2)}, u32[]{:S(2)}) %collective-permute-start.5) | collective-permute-done | bytes 786464 | tf_op jit(solution)/shard_map/ppermute | solution.py:317
  89.6 2.7 %all-to-all-done.1.first = bf16[4,768,512]{2,1,0:T(8,128)(2,1)} async-done(((bf16[4,768,512]{2,1,0:T(8,128)(2,1)}), bf16[4,768,512]{2,1,0:T(8,128)(2,1)}, u32[]{:S(2)}, u32[]{:S(2)}) %all-to-all-start.1) | async-done | bytes 3145760 | tf_op jit(solution)/shard_map/all_to_all | solution.py:369
  92.2 3.8 %collective-permute-start.6 = (bf16[4,768,512]{2,1,0:T(8,128)(2,1)}, bf16[4,768,512]{2,1,0:T(8,128)(2,1)}, u32[]{:S(2)}, u32[]{:S(2)}) collective-permute-start(bf16[4,768,512]{2,1,0:T(8,128)(2,1)} %all-to-all-done.1.first), channel_id=1, source_target_pairs={{0,16},{16,0},{1,17},{17,1},{2,18},{18,2},{3,19},{19,3},{4,20},{20... | collective-permute-start | bytes 9437192 | tf_op jit(solution)/shard_map/ppermute | solution.py:317
  96.2 1.2 fusion.19.refs_5_
  97.4 6.1 %partial.1.refs_0_ = f32[512,640]{1,0:T(8,128)S(1)} custom-call(s32[3]{0:T(128)S(1)} %pad_add_fusion.place_ref, bf16[4,768,512]{2,1,0:T(8,128)(2,1)} %all-to-all-done.1.first, bf16[4,768,128]{2,1,0:T(8,128)(2,1)S(1)} %pad_maximum_fusion.1.second, bf16[8,512,768]{2,1,0:T(8,128)(2,1)} %patches.1.patch_ref), custom_call_target="tpu_custom_call" | custom-call | flops 2013265920 | bytes 8388608 | tf_op jit(solution)/shard_map/partial/pallas_call | solution.py:225
  103.5 1.0 copy-done
  104.6 8.7 %forward.1 = (bf16[256,640]{1,0:T(8,128)(2,1)}, bf16[256,640]{1,0:T(8,128)(2,1)S(1)}, bf16[384,640]{1,0:T(8,128)(2,1)S(1)}, bf16[384,640]{1,0:T(8,128)(2,1)S(1)}) custom-call(s32[3]{0:T(128)S(1)} %pad_add_fusion.place_ref, bf16[4,768,512]{2,1,0:T(8,128)(2,1)} %collective-permute-done.6.first.other_first, ...), custom_call_target="tpu_custom_call" | custom-call | flops 4026531840 | bytes 20971520 | tf_op jit(solution)/shard_map/forward/pallas_call | solution.py:245
  113.3 1.9 %collective-permute-start.7 = (bf16[384,640]{1,0:T(8,128)(2,1)S(1)}, bf16[384,640]{1,0:T(8,128)(2,1)S(1)}, u32[]{:S(2)}, u32[]{:S(2)}) collective-permute-start(bf16[384,640]{1,0:T(8,128)(2,1)S(1)} %get-tuple-element.32), channel_id=1, source_target_pairs={{0,16},{16,0},{1,17},{17,1},{2,18},{18,2},{3,19},{19,3},{4,20},{20... | collective-permute-start | bytes 1474568 | tf_op jit(solution)/shard_map/ppermute | solution.py:317
  115.2 1.8 %collective-permute-done.7 = bf16[384,640]{1,0:T(8,128)(2,1)S(1)} collective-permute-done((bf16[384,640]{1,0:T(8,128)(2,1)S(1)}, bf16[384,640]{1,0:T(8,128)(2,1)S(1)}, u32[]{:S(2)}, u32[]{:S(2)}) %collective-permute-start.7) | collective-permute-done | bytes 491552 | tf_op jit(solution)/shard_map/ppermute | solution.py:317
  118.0 5.2 %all-to-all-start.2 = ((bf16[16,24,640]{2,1,0:T(8,128)(2,1)}), bf16[16,24,640]{2,1,0:T(8,128)(2,1)S(1)}, u32[]{:S(2)}, u32[]{:S(2)}) async-start(bf16[16,24,640]{2,1,0:T(8,128)(2,1)} %bitcast.20), calls=%async_computation.2 | async-start | bytes 983040 | tf_op jit(solution)/shard_map/all_to_all | solution.py:311
  123.2 5.0 %collective-permute-start.9 = (bf16[128,640]{1,0:T(8,128)(2,1)S(1)}, bf16[128,640]{1,0:T(8,128)(2,1)S(1)}, u32[]{:S(2)}, u32[]{:S(2)}) collective-permute-start(bf16[128,640]{1,0:T(8,128)(2,1)S(1)} %get-tuple-element.41), channel_id=1, source_target_pairs={{1,0},{2,1},{3,2},{4,3},{5,4},{6,5},{7,6},{8,7},{9,8},{10,9},{11,1... | collective-permute-start | bytes 491528 | tf_op jit(solution)/shard_map/ppermute | solution.py:323
  128.1 4.2 %collective-permute-start.8 = (bf16[128,640]{1,0:T(8,128)(2,1)S(1)}, bf16[128,640]{1,0:T(8,128)(2,1)S(1)}, u32[]{:S(2)}, u32[]{:S(2)}) collective-permute-start(bf16[128,640]{1,0:T(8,128)(2,1)S(1)} %get-tuple-element.42), channel_id=1, source_target_pairs={{0,1},{1,2},{2,3},{3,4},{4,5},{5,6},{6,7},{7,8},{8,9},{9,10},{10,1... | collective-permute-start | bytes 491528 | tf_op jit(solution)/shard_map/ppermute | solution.py:322
  132.4 6.4 %collective-permute-done.9 = bf16[128,640]{1,0:T(8,128)(2,1)S(1)} collective-permute-done((bf16[128,640]{1,0:T(8,128)(2,1)S(1)}, bf16[128,640]{1,0:T(8,128)(2,1)S(1)}, u32[]{:S(2)}, u32[]{:S(2)}) %collective-permute-start.9) | collective-permute-done | bytes 163872 | tf_op jit(solution)/shard_map/ppermute | solution.py:323
  138.8 8.5 %collective-permute-done.8 = bf16[128,640]{1,0:T(8,128)(2,1)S(1)} collective-permute-done((bf16[128,640]{1,0:T(8,128)(2,1)S(1)}, bf16[128,640]{1,0:T(8,128)(2,1)S(1)}, u32[]{:S(2)}, u32[]{:S(2)}) %collective-permute-start.8) | collective-permute-done | bytes 163872 | tf_op jit(solution)/shard_map/ppermute | solution.py:322
  148.2 11.7 %all-to-all-start.3 = ((bf16[16,24,640]{2,1,0:T(8,128)(2,1)}), bf16[16,24,640]{2,1,0:T(8,128)(2,1)S(1)}, u32[]{:S(2)}, u32[]{:S(2)}) async-start(bf16[16,24,640]{2,1,0:T(8,128)(2,1)} %broadcast_in_dim.11), calls=%async_computation.3 | async-start | bytes 983040 | tf_op jit(solution)/shard_map/all_to_all | solution.py:396
  159.9 9.8 %backward.1 = bf16[256,640]{1,0:T(8,128)(2,1)} custom-call(s32[3]{0:T(128)S(1)} %pad_add_fusion.place_ref, bf16[4,768,512]{2,1,0:T(8,128)(2,1)} %all-to-all-done.1.first, bf16[4,768,128]{2,1,0:T(8,128)(2,1)S(1)} %pad_maximum_fusion.1.second, bf16[4,768,512]{2,1,0:T(8,128)(2,1)} %collective-permute-done.6.first.other_first, ...), custom_call_target="tpu_custom_call" | custom-call | flops 2013265920 | bytes 31457280 | tf_op jit(solution)/shard_map/backward/pallas_call | solution.py:278
  169.7 5.2 %all-to-all-done.3 = bf16[16,24,640]{2,1,0:T(8,128)(2,1)S(1)} async-done(((bf16[16,24,640]{2,1,0:T(8,128)(2,1)}), bf16[16,24,640]{2,1,0:T(8,128)(2,1)S(1)}, u32[]{:S(2)}, u32[]{:S(2)}) %all-to-all-start.3) | async-done | bytes 491552 | tf_op jit(solution)/shard_map/all_to_all | solution.py:396
  175.0 3.6 %collective-permute-start.10 = (f32[24,640]{1,0:T(8,128)S(1)}, f32[24,640]{1,0:T(8,128)S(1)}, u32[]{:S(2)}, u32[]{:S(2)}) collective-permute-start(f32[24,640]{1,0:T(8,128)S(1)} %convert_reduce_fusion), channel_id=1, source_target_pairs={{0,16},{16,0},{1,17},{17,1},{2,18},{18,2},{3,19},{19,3},{4,20},{20... | collective-permute-start | bytes 184328 | tf_op jit(solution)/shard_map/ppermute | solution.py:317
  (53 shorter events, 5.6 us)
Async XLA Ops:
  3.9 44.8 %all-to-all-start = ((bf16[16,48,640]{2,1,0:T(8,128)(2,1)}), bf16[16,48,640]{2,1,0:T(8,128)(2,1)S(1)}, u32[]{:S(2)}, u32[]{:S(2)}) async-start(bf16[16,48,640]{2,1,0:T(8,128)(2,1)} %bitcast.8), calls=%async_computation | async-start | bytes 1966080 | tf_op jit(solution)/shard_map/all_to_all | solution.py:311
  50.7 5.3 %copy-start.2 = (bf16[1,4,64,640]{3,2,1,0:T(8,128)(2,1)S(1)}, bf16[1,4,64,640]{3,2,1,0:T(8,128)(2,1)}, u32[]{:S(2)}) copy-start(bf16[1,4,64,640]{3,2,1,0:T(8,128)(2,1)} %param.5) | copy-start | bytes 983044
  50.7 41.5 %all-to-all-start.1 = ((bf16[4,768,512]{2,1,0:T(8,128)(2,1)}), bf16[4,768,512]{2,1,0:T(8,128)(2,1)}, u32[]{:S(2)}, u32[]{:S(2)}) async-start(bf16[4,768,512]{2,1,0:T(8,128)(2,1)} %broadcast_in_dim.10), calls=%async_computation.1 | async-start | bytes 6291456 | tf_op jit(solution)/shard_map/all_to_all | solution.py:369
  56.1 28.8 %copy-start.1 = (bf16[640,1024]{1,0:T(8,128)(2,1)}, bf16[640,1024]{1,0:T(8,128)(2,1)S(1)}, u32[]{:S(2)}) copy-start(bf16[640,1024]{1,0:T(8,128)(2,1)S(1)} %fusion.9.spread_ref.refs_4_) | copy-start | bytes 3932164
  56.1 17.4 %collective-permute-start = (bf16[128,640]{1,0:T(8,128)(2,1)S(1)}, bf16[128,640]{1,0:T(8,128)(2,1)S(1)}, u32[]{:S(2)}, u32[]{:S(2)}) collective-permute-start(bf16[128,640]{1,0:T(8,128)(2,1)S(1)} %get-tuple-element.43), channel_id=1, source_target_pairs={{0,1},{1,2},{2,3},{3,4},{4,5},{5,6},{6,7},{7,8},{8,9},{9,10},{10,1... | collective-permute-start | bytes 491528 | tf_op jit(solution)/shard_map/ppermute | solution.py:322
  58.0 22.4 %collective-permute-start.1 = (bf16[128,640]{1,0:T(8,128)(2,1)S(1)}, bf16[128,640]{1,0:T(8,128)(2,1)S(1)}, u32[]{:S(2)}, u32[]{:S(2)}) collective-permute-start(bf16[128,640]{1,0:T(8,128)(2,1)S(1)} %get-tuple-element.44), channel_id=1, source_target_pairs={{1,0},{2,1},{3,2},{4,3},{5,4},{6,5},{7,6},{8,7},{9,8},{10,9},{11,1... | collective-permute-start | bytes 491528 | tf_op jit(solution)/shard_map/ppermute | solution.py:323
  66.3 18.6 %collective-permute-start.4 = (bf16[768,128]{1,0:T(8,128)(2,1)S(1)}, bf16[768,128]{1,0:T(8,128)(2,1)S(1)}, u32[]{:S(2)}, u32[]{:S(2)}) collective-permute-start(bf16[768,128]{1,0:T(8,128)(2,1)S(1)} %pad_maximum_fusion.5), channel_id=1, source_target_pairs={{14,0},{30,16},{0,2},{16,18},{2,4},{18,20},{4,6},{20,22},{6,8},{22... | collective-permute-start | bytes 589832 | tf_op jit(solution)/shard_map/ppermute | solution.py:303
  68.2 16.6 %collective-permute-start.3 = (bf16[768,128]{1,0:T(8,128)(2,1)S(1)}, bf16[768,128]{1,0:T(8,128)(2,1)S(1)}, u32[]{:S(2)}, u32[]{:S(2)}) collective-permute-start(bf16[768,128]{1,0:T(8,128)(2,1)S(1)} %pad_maximum_fusion.5), channel_id=1, source_target_pairs={{4,0},{28,16},{6,2},{30,18},{8,4},{16,20},{10,6},{18,22},{12,8},{2... | collective-permute-start | bytes 589832 | tf_op jit(solution)/shard_map/ppermute | solution.py:303
  71.0 13.9 %collective-permute-start.2 = (bf16[768,128]{1,0:T(8,128)(2,1)S(1)}, bf16[768,128]{1,0:T(8,128)(2,1)S(1)}, u32[]{:S(2)}, u32[]{:S(2)}) collective-permute-start(bf16[768,128]{1,0:T(8,128)(2,1)S(1)} %pad_maximum_fusion.5), channel_id=1, source_target_pairs={{2,0},{18,16},{4,2},{20,18},{6,4},{22,20},{8,6},{24,22},{10,8},{26... | collective-permute-start | bytes 589832 | tf_op jit(solution)/shard_map/ppermute | solution.py:303
  85.0 4.6 %collective-permute-start.5 = (bf16[4,768,128]{2,1,0:T(8,128)(2,1)S(1)}, bf16[4,768,128]{2,1,0:T(8,128)(2,1)S(1)}, u32[]{:S(2)}, u32[]{:S(2)}) collective-permute-start(bf16[4,768,128]{2,1,0:T(8,128)(2,1)S(1)} %pad_maximum_fusion.1.second), channel_id=1, source_target_pairs={{0,16},{16,0},{1,17},{17,1},{2,18},{18,2},{3,19},{19,3},{4,20},{20... | collective-permute-start | bytes 2359304 | tf_op jit(solution)/shard_map/ppermute | solution.py:317
  92.2 12.3 %collective-permute-start.6 = (bf16[4,768,512]{2,1,0:T(8,128)(2,1)}, bf16[4,768,512]{2,1,0:T(8,128)(2,1)}, u32[]{:S(2)}, u32[]{:S(2)}) collective-permute-start(bf16[4,768,512]{2,1,0:T(8,128)(2,1)} %all-to-all-done.1.first), channel_id=1, source_target_pairs={{0,16},{16,0},{1,17},{17,1},{2,18},{18,2},{3,19},{19,3},{4,20},{20... | collective-permute-start | bytes 9437192 | tf_op jit(solution)/shard_map/ppermute | solution.py:317
  97.4 7.2 %copy-start.3 = (bf16[1,4,64,640]{3,2,1,0:T(8,128)(2,1)S(1)}, bf16[1,4,64,640]{3,2,1,0:T(8,128)(2,1)}, u32[]{:S(2)}) copy-start(bf16[1,4,64,640]{3,2,1,0:T(8,128)(2,1)} %param.6) | copy-start | bytes 983044
  97.4 7.2 %copy-start.4 = (bf16[640,640]{1,0:T(8,128)(2,1)S(1)}, bf16[640,640]{1,0:T(8,128)(2,1)}, u32[]{:S(2)}) copy-start(bf16[640,640]{1,0:T(8,128)(2,1)} %refs_4_.1) | copy-start | bytes 2457604
  103.5 1.1 copy-start
  113.3 3.8 %collective-permute-start.7 = (bf16[384,640]{1,0:T(8,128)(2,1)S(1)}, bf16[384,640]{1,0:T(8,128)(2,1)S(1)}, u32[]{:S(2)}, u32[]{:S(2)}) collective-permute-start(bf16[384,640]{1,0:T(8,128)(2,1)S(1)} %get-tuple-element.32), channel_id=1, source_target_pairs={{0,16},{16,0},{1,17},{17,1},{2,18},{18,2},{3,19},{19,3},{4,20},{20... | collective-permute-start | bytes 1474568 | tf_op jit(solution)/shard_map/ppermute | solution.py:317
  118.0 29.3 %all-to-all-start.2 = ((bf16[16,24,640]{2,1,0:T(8,128)(2,1)}), bf16[16,24,640]{2,1,0:T(8,128)(2,1)S(1)}, u32[]{:S(2)}, u32[]{:S(2)}) async-start(bf16[16,24,640]{2,1,0:T(8,128)(2,1)} %bitcast.20), calls=%async_computation.2 | async-start | bytes 983040 | tf_op jit(solution)/shard_map/all_to_all | solution.py:311
  123.2 15.6 %collective-permute-start.9 = (bf16[128,640]{1,0:T(8,128)(2,1)S(1)}, bf16[128,640]{1,0:T(8,128)(2,1)S(1)}, u32[]{:S(2)}, u32[]{:S(2)}) collective-permute-start(bf16[128,640]{1,0:T(8,128)(2,1)S(1)} %get-tuple-element.41), channel_id=1, source_target_pairs={{1,0},{2,1},{3,2},{4,3},{5,4},{6,5},{7,6},{8,7},{9,8},{10,9},{11,1... | collective-permute-start | bytes 491528 | tf_op jit(solution)/shard_map/ppermute | solution.py:323
  128.1 19.1 %collective-permute-start.8 = (bf16[128,640]{1,0:T(8,128)(2,1)S(1)}, bf16[128,640]{1,0:T(8,128)(2,1)S(1)}, u32[]{:S(2)}, u32[]{:S(2)}) collective-permute-start(bf16[128,640]{1,0:T(8,128)(2,1)S(1)} %get-tuple-element.42), channel_id=1, source_target_pairs={{0,1},{1,2},{2,3},{3,4},{4,5},{5,6},{6,7},{7,8},{8,9},{9,10},{10,1... | collective-permute-start | bytes 491528 | tf_op jit(solution)/shard_map/ppermute | solution.py:322
  148.2 26.7 %all-to-all-start.3 = ((bf16[16,24,640]{2,1,0:T(8,128)(2,1)}), bf16[16,24,640]{2,1,0:T(8,128)(2,1)S(1)}, u32[]{:S(2)}, u32[]{:S(2)}) async-start(bf16[16,24,640]{2,1,0:T(8,128)(2,1)} %broadcast_in_dim.11), calls=%async_computation.3 | async-start | bytes 983040 | tf_op jit(solution)/shard_map/all_to_all | solution.py:396
  175.0 4.5 %collective-permute-start.10 = (f32[24,640]{1,0:T(8,128)S(1)}, f32[24,640]{1,0:T(8,128)S(1)}, u32[]{:S(2)}, u32[]{:S(2)}) collective-permute-start(f32[24,640]{1,0:T(8,128)S(1)} %convert_reduce_fusion), channel_id=1, source_target_pairs={{0,16},{16,0},{1,17},{17,1},{2,18},{18,2},{3,19},{19,3},{4,20},{20... | collective-permute-start | bytes 184328 | tf_op jit(solution)/shard_map/ppermute | solution.py:317
